TPU v7x, 32 devices: a whole 2x2x4 slice. The times are simulated.
32 devices in a mesh: gx: 2 (over y), gy: 4 (over z), ba: 4 (over x, core).
Axes of the slice: x: 2, y: 2, z: 4, core: 2. Of those that a mesh axis runs over, the one named last changes fastest.
Arguments:
- moved_fields: float32 [2, 4, 4, 4, 4, 4096], P('gx', 'gy', 'ba'), may hold values from -0.1 to 1.4, as said below
- send_slot: int32 [2, 4, 4, 4, 1], P('gx', 'gy', 'ba'), may hold values from -1 to 3, as said below
- recv_index: int32 [2, 4, 4, 2], P('gx', 'gy', 'ba'), may hold values from 0 to 3, as said below
- site_kind: int32 [32, 64, 128], P('gx', 'gy', 'ba'), may hold values from 0 to 3
Outputs:
- distributions: float32 [19, 32, 64, 128], P(None, 'gx', 'gy', 'ba')
Inputs may be any that keep to these rules, and one draw needn't show every extreme that they name: Blocks move only between devices with the same gx and ba. Within such a group, the live entries of one device's send_slot are distinct slots; the entry [p, c] is live exactly when some device p' = p of the group has recv_index p_sender + c naming this device, and every device receives exactly 2 blocks, each from one live entry. A device sends at most 1 block to one peer; the number of live slots of a device varies. `recv_index`: entries are distinct within a device and consistent with send_slot as stated there. `moved_fields`: component 0 is the density, between 0.6 and 1.4; components 1 to 3 are velocities between -0.1 and 0.1; slots that no live send_slot entry names hold values of the same kind.
All inputs are finite; a program needn't handle non-finite values.
Results may differ from a plain program's by a relative error of at most 0.0003.
Values sent between devices are 32-bit elements; how exact they have to be, the bound alone decides.
A program may use at most 64 MiB of HBM per device.

v0:
```python
import functools

import jax
import jax.numpy as jnp
from jax import lax
from jax.experimental import pallas as pl
from jax.experimental.pallas import tpu as pltpu
from jax.sharding import PartitionSpec as P

STEPS = 4
HALO = STEPS
PAIRS = (
    (1, 0, 0),
    (0, 1, 0),
    (0, 0, 1),
    (1, 1, 0),
    (1, -1, 0),
    (1, 0, 1),
    (1, 0, -1),
    (0, 1, 1),
    (0, 1, -1),
)
VELOCITIES = ((0, 0, 0),) + tuple(
    tuple(sign * part for part in vector) for vector in PAIRS for sign in (1, -1)
)
WEIGHTS = (1.0 / 3.0,) + (1.0 / 18.0,) * 6 + (1.0 / 36.0,) * 12
RELAX_RATE = 1.25
INLET_SPEED = 0.05
SUBLANES = 8
LANES = 128


def padded_2(array, sides, width):
    for axis, dim in sides:
        devices, length = (lax.axis_size(axis), array.shape[dim])
        up = [(i, (i + 1) % devices) for i in range(devices)]
        down = [(j, i) for i, j in up]
        last = lax.slice_in_dim(array, length - width, length, axis=dim)
        initial = lax.slice_in_dim(array, 0, width, axis=dim)
        before = lax.ppermute(last, axis, up)
        after = lax.ppermute(initial, axis, down)
        array = jnp.concatenate([before, array, after], axis=dim)
    return array


def dotted(vector, speeds):
    running = None
    for sign_value, component in zip(vector, speeds):
        if sign_value > 0:
            running = component if running is None else running + component
        elif sign_value < 0:
            running = -component if running is None else running - component
    return running


def row_ids():
    return lax.broadcasted_iota(jnp.int32, (SUBLANES, LANES), 0)


def shifted(plane, rows, stride, step_y, step_z):
    if step_y:
        rolled = pltpu.roll(plane, step_y % SUBLANES, 0)
        crossed = pltpu.roll(rolled, (step_y * stride) % LANES, 1)
        plane = jnp.where(rows == (0 if step_y > 0 else SUBLANES - 1), crossed, rolled)
    if step_z:
        plane = pltpu.roll(plane, step_z % LANES, 1)
    return plane


def squared_base(speeds):
    return 1.0 - (1.0 / 6.0) * (
        speeds[0] * speeds[0] + speeds[1] * speeds[1] + speeds[2] * speeds[2]
    )


def start_plane(fields, kind):
    wall, inlet = kind == 1.0, kind == 2.0
    factor = jnp.where(kind <= 1.0, fields[0], 1.0)
    scale = jnp.where(wall, -3.0, jnp.where(inlet, 0.0, 3.0))
    speeds = [scale * fields[axis] for axis in (1, 2, 3)]
    speeds[2] = jnp.where(inlet, 3.0 * INLET_SPEED, speeds[2])
    base = squared_base(speeds)
    result = [WEIGHTS[0] * factor * base]
    weighted = {w: w * factor for w in set(WEIGHTS[1:])}
    for pair_id, vector in enumerate(PAIRS):
        w = weighted[WEIGHTS[1 + 2 * pair_id]]
        projected = dotted(vector, speeds)
        even = w * (base + 0.5 * projected * projected)
        odd = w * projected
        result += [even + odd, even - odd]
    return result


def collide_plane(populations, kind):
    fluid, wall, inlet = kind == 0.0, kind == 1.0, kind == 2.0
    sums = [populations[i] + populations[i + 1] for i in range(1, 19, 2)]
    differences = [populations[i] - populations[i + 1] for i in range(1, 19, 2)]
    density = populations[0]
    for member in sums:
        density = density + member
    triple = 3.0 / density
    speeds = []
    for axis in range(3):
        momentum = dotted([vector[axis] for vector in PAIRS], differences)
        speeds.append(jnp.where(wall | inlet, 0.0, momentum * triple))
    speeds[2] = jnp.where(inlet, 3.0 * INLET_SPEED, speeds[2])
    base = squared_base(speeds)
    factor = jnp.where(fluid, RELAX_RATE * density, jnp.where(wall, 0.0, 1.0))
    keep = jnp.where(fluid, 1.0 - RELAX_RATE, jnp.where(wall, 1.0, 0.0))
    half_even = 0.5 * keep
    half_odd = jnp.where(wall, -0.5, half_even)
    result = [keep * populations[0] + WEIGHTS[0] * factor * base]
    weighted = {w: w * factor for w in set(WEIGHTS[1:])}
    for pair_id, vector in enumerate(PAIRS):
        w = weighted[WEIGHTS[1 + 2 * pair_id]]
        projected = dotted(vector, speeds)
        even = half_even * sums[pair_id] + w * (base + 0.5 * projected * projected)
        odd = half_odd * differences[pair_id] + w * projected
        result += [even + odd, even - odd]
    return result


def lattice_kernel(fields_ref, out_ref, first, second):
    planes = fields_ref.shape[1]
    extent_y, extent_z = out_ref.shape[2:]
    stride = extent_z + 2 * HALO
    rows = row_ids()

    def begin(x, carry):
        fields = [fields_ref[i, x] for i in range(5)]
        for i, member in enumerate(start_plane(fields, fields[4])):
            first[i, x] = member
        return carry

    lax.fori_loop(0, planes, begin, 0)
    source, target = first, second
    for step in range(1, STEPS):

        def advance(x, carry, source=source, target=target):
            pulled = [
                shifted(source[i, x - v[0]], rows, stride, v[1], v[2])
                for i, v in enumerate(VELOCITIES)
            ]
            for i, member in enumerate(collide_plane(pulled, fields_ref[4, x])):
                target[i, x] = member
            return carry

        lax.fori_loop(step, planes - step, advance, 0)
        source, target = target, source

    def finish(x, carry):
        for i, v in enumerate(VELOCITIES):
            plane = source[i, x + HALO - v[0]]
            offset = HALO - v[1]
            plane = pltpu.roll(plane, SUBLANES - offset, 0)
            crossed = pltpu.roll(plane, LANES - stride, 1)
            plane = jnp.where(rows < SUBLANES - offset, plane, crossed)
            for group in range(extent_y // SUBLANES):
                part = pltpu.roll(plane, LANES - (group * stride + HALO - v[2]), 1)
                out_ref[i, x, pl.ds(group * SUBLANES, SUBLANES), :] = part[:, :extent_z]
        return carry

    lax.fori_loop(0, out_ref.shape[1], finish, 0)


def lattice(fields, extents):
    planes = fields.shape[1]
    return pl.pallas_call(
        lattice_kernel,
        out_shape=jax.ShapeDtypeStruct((19,) + tuple(extents), jnp.float32),
        in_specs=[pl.BlockSpec(memory_space=pltpu.VMEM)],
        out_specs=pl.BlockSpec(memory_space=pltpu.VMEM),
        scratch_shapes=[pltpu.VMEM((19, planes, SUBLANES, LANES), jnp.float32)] * 2,
        compiler_params=pltpu.CompilerParams(vmem_limit_bytes=24 * 1024 * 1024),
        name="lattice",
    )(fields)


def on_device(moved_fields, send_slot, recv_index, site_kind):
    held_blocks = moved_fields[0, 0, 0]
    wanted = send_slot[0, 0, 0]
    peer_count = wanted.shape[0]
    per_peer = wanted.shape[1]
    flat_wanted = wanted.reshape(peer_count * per_peer)
    picked = jnp.take(held_blocks, jnp.maximum(flat_wanted, 0), axis=0)
    picked = jnp.where((flat_wanted >= 0)[:, None, None], picked, 0.0)
    outgoing = picked.reshape(peer_count, per_peer, held_blocks.shape[1], held_blocks.shape[2])
    arrived = lax.all_to_all(outgoing, "gy", split_axis=0, concat_axis=0, tiled=True)
    arrived = arrived.reshape(peer_count * per_peer, held_blocks.shape[1], held_blocks.shape[2])
    placed = jnp.take(arrived, recv_index[0, 0, 0], axis=0)
    block_edge = site_kind.shape[0]
    blocks_here = placed.shape[0]
    placed = placed.reshape(blocks_here, 4, block_edge, block_edge, block_edge)
    placed = placed.transpose(1, 2, 3, 0, 4).reshape(
        4, block_edge, block_edge, blocks_here * block_edge
    )
    fields = jnp.concatenate([placed, site_kind[None].astype(jnp.float32)])
    fields = padded_2(fields, (("gx", 1), ("gy", 2), ("ba", 3)), HALO)
    parts, extent_x, extent_y, extent_z = fields.shape
    groups = extent_y // SUBLANES
    packed = fields.reshape(parts, extent_x, groups, SUBLANES, extent_z)
    packed = packed.transpose(0, 1, 3, 2, 4).reshape(parts, extent_x, SUBLANES, -1)
    packed = jnp.pad(packed, ((0, 0), (0, 0), (0, 0), (0, LANES - packed.shape[3])))
    return lattice(packed, site_kind.shape)


def solution(mesh):
    return jax.shard_map(
        on_device,
        mesh=mesh,
        in_specs=(
            P("gx", "gy", "ba", None, None, None),
            P("gx", "gy", "ba", None, None),
            P("gx", "gy", "ba", None),
            P("gx", "gy", "ba"),
        ),
        out_specs=P(None, "gx", "gy", "ba"),
        check_vma=False,
    )
```

profile of v0, /device:TPU:1, one launch (start us, length us, event | category | flops | bytes accessed | tf_op | source)
XLA Modules:
  0.0 73.9 jit_solution(3626946774640688401)
XLA Ops:
  0.0 0.0 copy-start
  0.0 0.0 copy-start.2
  0.0 0.0 copy-start.1
  0.0 0.7 maximum_bitcast_fusion.1
  0.7 0.7 compare_bitcast_fusion.1
  1.4 0.0 copy-done
  1.4 0.7 gather_fusion
  2.1 0.8 %fusion.1 = f32[4,1,4,4096]{3,2,1,0:T(4,128)} fusion(f32[4,4,4096]{2,1,0:T(4,128)S(1)} %gather_fusion, pred[4]{0:T(512)(128)(4,1)S(1)} %get-tuple-element.12, pred[4]{0:T(512)(128)(4,1)S(1)} %get-tuple-element.11), kind=kLoop, calls=%fused_computation.7 | loop fusion | flops 131072 | bytes 524296 | tf_op jit(solution)/shard_map/jit(_where)/select_n | solution.py:186
  2.9 5.4 %all-to-all-start = ((f32[4,1,4,4096]{3,2,1,0:T(4,128)}), f32[4,1,4,4096]{3,2,1,0:T(4,128)S(1)}, u32[]{:S(2)}, u32[]{:S(2)}) async-start(f32[4,1,4,4096]{3,2,1,0:T(4,128)} %fusion.1), calls=%async_computation | async-start | bytes 524288 | tf_op jit(solution)/shard_map/all_to_all | solution.py:188
  8.4 0.0 copy-done.2
  8.4 0.0 copy-done.1
  8.4 7.5 %all-to-all-done = f32[4,1,4,4096]{3,2,1,0:T(4,128)S(1)} async-done(((f32[4,1,4,4096]{3,2,1,0:T(4,128)}), f32[4,1,4,4096]{3,2,1,0:T(4,128)S(1)}, u32[]{:S(2)}, u32[]{:S(2)}) %all-to-all-start) | async-done | bytes 262176 | tf_op jit(solution)/shard_map/all_to_all | solution.py:188
  15.9 0.6 gather_fusion.1
  16.6 0.4 gather.15
  16.9 1.0 %fusion = f32[4,16,16,2,16]{4,3,2,1,0:T(2,128)S(1)} fusion(f32[2,4,16,16,16]{4,3,2,1,0:T(8,128)S(1)} %gather.15, pred[2]{0:T(512)(128)(4,1)S(1)} %compare_and_fusion), kind=kLoop, calls=%fused_computation.5 | loop fusion | flops 32768 | bytes 262146 | tf_op jit(solution)/shard_map/transpose | solution.py:194
  18.0 0.6 reshape.90
  18.6 1.3 %collective-permute-start = (f32[5,4,16,32]{3,2,1,0:T(8,128)S(1)}, f32[5,4,16,32]{3,2,1,0:T(8,128)S(1)}, u32[]{:S(2)}, u32[]{:S(2)}) collective-permute-start(f32[5,4,16,32]{3,2,1,0:T(8,128)S(1)} %get-tuple-element.9), channel_id=1, source_target_pairs={{0,16},{16,0},{1,17},{17,1},{2,18},{18,2},{3,19},{19,3},{4,20},{20... | collective-permute-start | bytes 122888 | tf_op jit(solution)/shard_map/ppermute | solution.py:40
  19.9 0.2 collective-permute-start.1
  20.1 2.7 %collective-permute-done = f32[5,4,16,32]{3,2,1,0:T(8,128)S(1)} collective-permute-done((f32[5,4,16,32]{3,2,1,0:T(8,128)S(1)}, f32[5,4,16,32]{3,2,1,0:T(8,128)S(1)}, u32[]{:S(2)}, u32[]{:S(2)}) %collective-permute-start) | collective-permute-done | bytes 40992 | tf_op jit(solution)/shard_map/ppermute | solution.py:40
  22.8 2.7 %collective-permute-done.1 = f32[5,4,16,32]{3,2,1,0:T(8,128)S(1)} collective-permute-done((f32[5,4,16,32]{3,2,1,0:T(8,128)S(1)}, f32[5,4,16,32]{3,2,1,0:T(8,128)S(1)}, u32[]{:S(2)}, u32[]{:S(2)}) %collective-permute-start.1) | collective-permute-done | bytes 40992 | tf_op jit(solution)/shard_map/ppermute | solution.py:41
  25.6 0.1 pad_maximum_fusion.4
  25.7 0.1 collective-permute-start.2
  25.8 3.2 %collective-permute-start.3 = (f32[5,24,4,32]{3,2,1,0:T(4,128)S(1)}, f32[5,24,4,32]{3,2,1,0:T(4,128)S(1)}, u32[]{:S(2)}, u32[]{:S(2)}) collective-permute-start(f32[5,24,4,32]{3,2,1,0:T(4,128)S(1)} %get-tuple-element.8), channel_id=1, source_target_pairs={{4,0},{8,4},{12,8},{0,12},{5,1},{9,5},{13,9},{1,13},{6,2},{10,6},{... | collective-permute-start | bytes 184328 | tf_op jit(solution)/shard_map/ppermute | solution.py:41
  29.0 3.7 %collective-permute-done.2 = f32[5,24,4,32]{3,2,1,0:T(4,128)S(1)} collective-permute-done((f32[5,24,4,32]{3,2,1,0:T(4,128)S(1)}, f32[5,24,4,32]{3,2,1,0:T(4,128)S(1)}, u32[]{:S(2)}, u32[]{:S(2)}) %collective-permute-start.2) | collective-permute-done | bytes 61472 | tf_op jit(solution)/shard_map/ppermute | solution.py:40
  32.7 2.2 %collective-permute-done.3 = f32[5,24,4,32]{3,2,1,0:T(4,128)S(1)} collective-permute-done((f32[5,24,4,32]{3,2,1,0:T(4,128)S(1)}, f32[5,24,4,32]{3,2,1,0:T(4,128)S(1)}, u32[]{:S(2)}, u32[]{:S(2)}) %collective-permute-start.3) | collective-permute-done | bytes 61472 | tf_op jit(solution)/shard_map/ppermute | solution.py:41
  35.0 0.3 pad_maximum_fusion
  35.3 1.6 %fusion.3 = (f32[5,24,24,4]{3,2,1,0:T(8,128)}, f32[5,24,24,4]{3,2,1,0:T(8,128)S(1)}) fusion(f32[5,24,24,32]{3,2,1,0:T(8,128)S(1)} %pad_maximum_fusion), kind=kLoop, calls=%fused_computation.24 | loop fusion | bytes 184320 | tf_op jit(solution)/shard_map/slice | solution.py:38
  36.9 2.1 %copy.8 = f32[5,24,24,4]{2,1,3,0:T(8,128)S(1)} copy(f32[5,24,24,4]{3,2,1,0:T(8,128)} %get-tuple-element.5) | data formatting | bytes 92160 | tf_op jit(solution)/shard_map/slice | solution.py:38
  39.0 5.6 %collective-permute-start.4 = (f32[5,24,24,4]{2,1,3,0:T(8,128)S(1)}, f32[5,24,24,4]{2,1,3,0:T(8,128)}, u32[]{:S(2)}, u32[]{:S(2)}) collective-permute-start(f32[5,24,24,4]{2,1,3,0:T(8,128)S(1)} %copy.8), channel_id=1, source_target_pairs={{0,1},{1,2},{2,3},{3,0},{4,5},{5,6},{6,7},{7,4},{8,9},{9,10},{10,1... | collective-permute-start | bytes 138248 | tf_op jit(solution)/shard_map/ppermute | solution.py:40
  44.6 1.5 %copy.9 = f32[5,24,24,4]{2,1,3,0:T(8,128)} copy(f32[5,24,24,4]{3,2,1,0:T(8,128)S(1)} %get-tuple-element.6) | data formatting | bytes 92160 | tf_op jit(solution)/shard_map/slice | solution.py:39
  46.1 0.0 collective-permute-start.5
  46.1 1.7 %collective-permute-done.4 = f32[5,24,24,4]{2,1,3,0:T(8,128)} collective-permute-done((f32[5,24,24,4]{2,1,3,0:T(8,128)S(1)}, f32[5,24,24,4]{2,1,3,0:T(8,128)}, u32[]{:S(2)}, u32[]{:S(2)}) %collective-permute-start.4) | collective-permute-done | bytes 46112 | tf_op jit(solution)/shard_map/ppermute | solution.py:40
  47.8 1.7 %copy.10 = f32[5,24,24,4]{3,2,1,0:T(8,128)S(1)} copy(f32[5,24,24,4]{2,1,3,0:T(8,128)} %collective-permute-done.4) | data formatting | bytes 92160 | tf_op jit(solution)/shard_map/ppermute | solution.py:40
  49.5 2.6 %collective-permute-done.5 = f32[5,24,24,4]{2,1,3,0:T(8,128)} collective-permute-done((f32[5,24,24,4]{2,1,3,0:T(8,128)}, f32[5,24,24,4]{2,1,3,0:T(8,128)}, u32[]{:S(2)}, u32[]{:S(2)}) %collective-permute-start.5) | collective-permute-done | bytes 46112 | tf_op jit(solution)/shard_map/ppermute | solution.py:41
  52.0 2.8 %copy.11 = f32[5,24,24,4]{3,2,1,0:T(8,128)} copy(f32[5,24,24,4]{2,1,3,0:T(8,128)} %collective-permute-done.5) | data formatting | bytes 92160 | tf_op jit(solution)/shard_map/ppermute | solution.py:41
  54.9 2.5 %maximum_bitcast_fusion = f32[5,24,8,3,40]{4,2,3,1,0:T(8,128)S(1)} fusion(f32[5,24,24,4]{3,2,1,0:T(8,128)} %copy.11, f32[5,24,4,32]{3,2,1,0:T(4,128)S(1)} %collective-permute-done.3, f32[5,4,16,32]{3,2,1,0:T(8,128)S(1)} %collective-permute-done.1, f32[1,16,16,32]{3,2,1,0:T(8,128)S(1)} %convert_bitcast_fusion, f32[4,16,16,32]{3,2,1,0:T(8,128)S(1)} %reshape.90, ...), kind=kLoop, calls=%fused_computation.3 | loop fusion | flops 806400 | bytes 921600 | tf_op jit(solution)/shard_map/transpose | solution.py:202
  57.3 0.6 copy.12
  57.9 0.8 %reshape.92 = f32[5,24,8,120]{3,2,1,0:T(8,128)S(1)} reshape(f32[5,24,8,3,40]{4,3,2,1,0:T(4,128)S(1)} %copy.12) | data formatting | bytes 921600 | tf_op jit(solution)/shard_map/reshape | solution.py:202
  58.7 15.2 %lattice.1 = f32[19,16,16,32]{3,2,1,0:T(8,128)} custom-call(f32[5,24,8,128]{3,2,1,0:T(8,128)S(1)} %pad.4.fields_ref), custom_call_target="tpu_custom_call" | custom-call | tf_op jit(solution)/shard_map/lattice/pallas_call | solution.py:168
  (7 shorter events, 0.1 us)
Async XLA Ops:
  0.0 1.4 %copy-start = (f32[1,1,1,4,4,4096]{5,4,3,2,1,0:T(4,128)S(1)}, f32[1,1,1,4,4,4096]{5,4,3,2,1,0:T(4,128)}, u32[]{:S(2)}) copy-start(f32[1,1,1,4,4,4096]{5,4,3,2,1,0:T(4,128)} %param.4) | copy-start | bytes 786436
  0.0 8.4 %copy-start.2 = (s32[1,1,1,2]{3,2,1,0:T(1,128)S(1)}, s32[1,1,1,2]{3,2,1,0:T(1,128)}, u32[]{:S(2)}) copy-start(s32[1,1,1,2]{3,2,1,0:T(1,128)} %param.6) | copy-start | bytes 28
  0.0 8.4 %copy-start.1 = (s32[16,16,32]{2,1,0:T(8,128)S(1)}, s32[16,16,32]{2,1,0:T(8,128)}, u32[]{:S(2)}) copy-start(s32[16,16,32]{2,1,0:T(8,128)} %param.7) | copy-start | bytes 98308
  2.9 13.0 %all-to-all-start = ((f32[4,1,4,4096]{3,2,1,0:T(4,128)}), f32[4,1,4,4096]{3,2,1,0:T(4,128)S(1)}, u32[]{:S(2)}, u32[]{:S(2)}) async-start(f32[4,1,4,4096]{3,2,1,0:T(4,128)} %fusion.1), calls=%async_computation | async-start | bytes 524288 | tf_op jit(solution)/shard_map/all_to_all | solution.py:188
  18.6 4.2 %collective-permute-start = (f32[5,4,16,32]{3,2,1,0:T(8,128)S(1)}, f32[5,4,16,32]{3,2,1,0:T(8,128)S(1)}, u32[]{:S(2)}, u32[]{:S(2)}) collective-permute-start(f32[5,4,16,32]{3,2,1,0:T(8,128)S(1)} %get-tuple-element.9), channel_id=1, source_target_pairs={{0,16},{16,0},{1,17},{17,1},{2,18},{18,2},{3,19},{19,3},{4,20},{20... | collective-permute-start | bytes 122888 | tf_op jit(solution)/shard_map/ppermute | solution.py:40
  19.9 5.7 %collective-permute-start.1 = (f32[5,4,16,32]{3,2,1,0:T(8,128)S(1)}, f32[5,4,16,32]{3,2,1,0:T(8,128)S(1)}, u32[]{:S(2)}, u32[]{:S(2)}) collective-permute-start(f32[5,4,16,32]{3,2,1,0:T(8,128)S(1)} %get-tuple-element.10), channel_id=1, source_target_pairs={{16,0},{0,16},{17,1},{1,17},{18,2},{2,18},{19,3},{3,19},{20,4},{4,... | collective-permute-start | bytes 122888 | tf_op jit(solution)/shard_map/ppermute | solution.py:41
  25.7 7.1 %collective-permute-start.2 = (f32[5,24,4,32]{3,2,1,0:T(4,128)S(1)}, f32[5,24,4,32]{3,2,1,0:T(4,128)S(1)}, u32[]{:S(2)}, u32[]{:S(2)}) collective-permute-start(f32[5,24,4,32]{3,2,1,0:T(4,128)S(1)} %get-tuple-element.7), channel_id=1, source_target_pairs={{0,4},{4,8},{8,12},{12,0},{1,5},{5,9},{9,13},{13,1},{2,6},{6,10},{... | collective-permute-start | bytes 184328 | tf_op jit(solution)/shard_map/ppermute | solution.py:40
  25.8 9.2 %collective-permute-start.3 = (f32[5,24,4,32]{3,2,1,0:T(4,128)S(1)}, f32[5,24,4,32]{3,2,1,0:T(4,128)S(1)}, u32[]{:S(2)}, u32[]{:S(2)}) collective-permute-start(f32[5,24,4,32]{3,2,1,0:T(4,128)S(1)} %get-tuple-element.8), channel_id=1, source_target_pairs={{4,0},{8,4},{12,8},{0,12},{5,1},{9,5},{13,9},{1,13},{6,2},{10,6},{... | collective-permute-start | bytes 184328 | tf_op jit(solution)/shard_map/ppermute | solution.py:41
  39.0 8.8 %collective-permute-start.4 = (f32[5,24,24,4]{2,1,3,0:T(8,128)S(1)}, f32[5,24,24,4]{2,1,3,0:T(8,128)}, u32[]{:S(2)}, u32[]{:S(2)}) collective-permute-start(f32[5,24,24,4]{2,1,3,0:T(8,128)S(1)} %copy.8), channel_id=1, source_target_pairs={{0,1},{1,2},{2,3},{3,0},{4,5},{5,6},{6,7},{7,4},{8,9},{9,10},{10,1... | collective-permute-start | bytes 138248 | tf_op jit(solution)/shard_map/ppermute | solution.py:40
  46.1 5.9 %collective-permute-start.5 = (f32[5,24,24,4]{2,1,3,0:T(8,128)}, f32[5,24,24,4]{2,1,3,0:T(8,128)}, u32[]{:S(2)}, u32[]{:S(2)}) collective-permute-start(f32[5,24,24,4]{2,1,3,0:T(8,128)} %copy.9), channel_id=1, source_target_pairs={{1,0},{2,1},{3,2},{0,3},{5,4},{6,5},{7,6},{4,7},{9,8},{10,9},{11,1... | collective-permute-start | bytes 138248 | tf_op jit(solution)/shard_map/ppermute | solution.py:41
where the time goes:
time: 74.3 us; the launch traced here: 73.9 us
  waiting for transfers between devices  23.1 us (31%)
  starting transfers between devices  15.9 us (21%)
  Pallas kernels  15.2 us (20%)
  local copies, waits for them, and re-layouts  13.4 us (18%)
  other arithmetic  6.14 us (8%)
    pallas_call x1, Pallas kernels, lattice(): pl.pallas_call(lattice_kernel, out_shape=jax.ShapeDtypeStruct((19,) + tup...  15.2 us
    ppermute x3, waiting for transfers between devices, padded_2(): before = lax.ppermute(last, axis, up)  8.09 us
    ppermute x3, waiting for transfers between devices, padded_2(): after = lax.ppermute(initial, axis, down)  7.54 us
    all_to_all x1, waiting for transfers between devices, on_device(): lax.all_to_all(outgoing, 'gy', split_axis=0, concat_axis=0, tiled=True)  7.5 us
    ppermute x3, starting transfers between devices, padded_2(): before = lax.ppermute(last, axis, up)  7.06 us
    all_to_all x1, starting transfers between devices, on_device(): lax.all_to_all(outgoing, 'gy', split_axis=0, concat_axis=0, tiled=True)  5.42 us
    slice x2, local copies, waits for them, and re-layouts, padded_2(): last = lax.slice_in_dim(array, length - width, length, axis=dim)  3.73 us
    ppermute x3, starting transfers between devices, padded_2(): after = lax.ppermute(initial, axis, down)  3.41 us
  transfers between devices with their start and end apart: 7, of which 7 were waited for; matrix products, arithmetic and copies ran while one was open for 4% of the time, Pallas kernels for 0%

commit v1 on v0

--- a/solution.py
+++ b/solution.py
@@ -28,19 +28,6 @@
 INLET_SPEED = 0.05
 SUBLANES = 8
 LANES = 128
-
-
-def padded_2(array, sides, width):
-    for axis, dim in sides:
-        devices, length = (lax.axis_size(axis), array.shape[dim])
-        up = [(i, (i + 1) % devices) for i in range(devices)]
-        down = [(j, i) for i, j in up]
-        last = lax.slice_in_dim(array, length - width, length, axis=dim)
-        initial = lax.slice_in_dim(array, 0, width, axis=dim)
-        before = lax.ppermute(last, axis, up)
-        after = lax.ppermute(initial, axis, down)
-        array = jnp.concatenate([before, array, after], axis=dim)
-    return array
 
 
 def dotted(vector, speeds):
@@ -176,32 +163,324 @@
     )(fields)
 
 
+def mesh_device(**moved):
+    return tuple(moved.get(axis, lax.axis_index(axis)) for axis in ("gx", "gy", "ba"))
+
+
+def remote(source, target, send_sem, recv_sem, device):
+    return pltpu.make_async_remote_copy(
+        src_ref=source,
+        dst_ref=target,
+        send_sem=send_sem,
+        recv_sem=recv_sem,
+        device_id=device,
+        device_id_type=pl.DeviceIdType.MESH,
+    )
+
+
+def grouped(low, high, rows, lanes, stride):
+    middle = pltpu.roll(jnp.where(rows < HALO, low, high), stride, 1)
+    last = pltpu.roll(high, 2 * stride, 1)
+    return jnp.where(lanes < stride, low, jnp.where(lanes < 2 * stride, middle, last))
+
+
+def gather_kernel(
+    moved_ref,
+    slot_ref,
+    index_ref,
+    kind_ref,
+    out_ref,
+    staged,
+    arrived,
+    chosen,
+    side_x,
+    kind_wide,
+    kind_x,
+    send_y,
+    side_y,
+    send_z,
+    side_z,
+    sent_sem,
+    arrived_sem,
+    halo_sent,
+    halo_arrived,
+):
+    extent_x, extent_y, extent_z = kind_ref.shape
+    blocks = chosen.shape[0]
+    edge = extent_z // blocks
+    stride = extent_z + 2 * HALO
+    planes = extent_x + 2 * HALO
+    rows = row_ids()
+    lanes = lax.broadcasted_iota(jnp.int32, (SUBLANES, LANES), 1)
+    me = {axis: lax.axis_index(axis) for axis in ("gx", "gy", "ba")}
+    size = {axis: lax.axis_size(axis) for axis in ("gx", "gy", "ba")}
+    up = {a: mesh_device(**{a: lax.rem(me[a] + 1, size[a])}) for a in me}
+    down = {a: mesh_device(**{a: lax.rem(me[a] + size[a] - 1, size[a])}) for a in me}
+    peers = [lax.rem(me["gy"] + offset, size["gy"]) for offset in range(size["gy"])]
+
+    barrier = pltpu.get_barrier_semaphore()
+    greeted = [mesh_device(gy=peer) for peer in peers[1:]]
+    greeted += [up["gx"], down["gx"], up["ba"], down["ba"]]
+    for device in greeted:
+        pl.semaphore_signal(
+            barrier, inc=1, device_id=device, device_id_type=pl.DeviceIdType.MESH
+        )
+    for offset in range(1, size["gy"]):
+        staged[offset] = moved_ref[jnp.maximum(slot_ref[peers[offset]], 0)]
+    pl.semaphore_wait(barrier, len(greeted))
+
+    moves = []
+    for offset in range(1, size["gy"]):
+        moves.append(
+            remote(
+                staged.at[offset],
+                arrived.at[me["gy"]],
+                sent_sem.at[offset],
+                arrived_sem.at[offset],
+                mesh_device(gy=peers[offset]),
+            )
+        )
+        moves[-1].start()
+    arrived[me["gy"]] = moved_ref[jnp.maximum(slot_ref[me["gy"]], 0)]
+
+    def halo(axis, number, low_source, high_source, target):
+        pair = [
+            remote(
+                high_source,
+                target.at[0],
+                halo_sent.at[2 * number],
+                halo_arrived.at[2 * number],
+                up[axis],
+            ),
+            remote(
+                low_source,
+                target.at[1],
+                halo_sent.at[2 * number + 1],
+                halo_arrived.at[2 * number + 1],
+                down[axis],
+            ),
+        ]
+        for copy in pair:
+            copy.start()
+        return pair
+
+    def lay_kind(x, carry):
+        parts = []
+        for half in range(2):
+            kind_wide[x, half, :, pl.ds(0, extent_z)] = kind_ref[
+                x, pl.ds(half * SUBLANES, SUBLANES), :
+            ].astype(jnp.float32)
+            wide = pltpu.roll(kind_wide[x, half], HALO, 0)
+            parts.append(pltpu.roll(wide, HALO, 1))
+        out_ref[4, x + HALO] = grouped(parts[0], parts[1], rows, lanes, stride)
+        return carry
+
+    lax.fori_loop(0, extent_x, lay_kind, 0)
+    kind_copies = halo(
+        "gx",
+        0,
+        out_ref.at[4, pl.ds(HALO, HALO)],
+        out_ref.at[4, pl.ds(extent_x, HALO)],
+        kind_x,
+    )
+
+    for move in moves:
+        move.wait_recv()
+    for block in range(blocks):
+        chosen[block] = arrived[index_ref[block]]
+
+    plane_size = edge * edge
+    layers = HALO * plane_size
+    x_copies = halo(
+        "gx",
+        1,
+        chosen.at[:, :, pl.ds(0, layers)],
+        chosen.at[:, :, pl.ds(extent_x * plane_size - layers, layers)],
+        side_x,
+    )
+
+    def lay_fields(read, x, target_x):
+        tiles = []
+        for block in range(2):
+            for half in range(2):
+                start = pl.multiple_of(x * plane_size + half * LANES, LANES)
+                tiles.append(read(block, pl.ds(start, LANES)))
+        quarter, half_lanes, whole = LANES // 4, LANES // 2, LANES
+        for part in range(4):
+            picked = []
+            for source, tile in enumerate(tiles):
+                row = jnp.broadcast_to(tile[part : part + 1], (SUBLANES, LANES))
+                turned = pltpu.roll(row, half_lanes, 1)
+                low_first = (rows >= HALO) == (source % 2 == 0)
+                picked.append(jnp.where(low_first, row, turned))
+            pairs = []
+            for block in range(2):
+                pair = jnp.where(lanes < half_lanes, picked[2 * block], picked[2 * block + 1])
+                shift = quarter if block else whole - quarter
+                turned = pltpu.roll(pair, shift, 1)
+                stays = ((rows & 2) == 0) == (block == 0)
+                pairs.append(jnp.where(stays, pair, turned))
+            joined = jnp.where((lanes & quarter) == 0, pairs[0], pairs[1])
+            joined = jnp.where((rows & 1) == 0, joined, pltpu.roll(joined, whole - edge, 1))
+            near = pltpu.roll(joined, HALO, 1)
+            far = pltpu.roll(joined, (HALO + edge - quarter) % whole, 1)
+            low = jnp.where((lanes & (half_lanes - 1)) < HALO + edge, near, far)
+            high = pltpu.roll(low, half_lanes, 1)
+            out_ref[part, target_x] = grouped(low, high, rows, lanes, stride)
+
+    def lay_own(x, carry):
+        lay_fields(lambda block, cut: chosen[block, :, cut], x, x + HALO)
+        return carry
+
+    lax.fori_loop(0, extent_x, lay_own, 0)
+    for copy in kind_copies:
+        copy.wait()
+    for copy in x_copies:
+        copy.wait_recv()
+
+    for side in range(2):
+        first_x = side * (extent_x + HALO)
+
+        def lay_side(x, carry, side=side, first_x=first_x):
+            lay_fields(lambda block, cut: side_x[side, block, :, cut], x, first_x + x)
+            out_ref[4, first_x + x] = kind_x[side, x]
+            return carry
+
+        lax.fori_loop(0, HALO, lay_side, 0)
+
+    per_y = 6
+    count_y = planes // per_y
+
+    def pack_y(index, carry):
+        part, first_x = index // count_y, (index % count_y) * per_y
+        own = [out_ref[part, first_x + k] for k in range(per_y)]
+        for side in range(2):
+            merged = []
+            for half in range(2):
+                total = None
+                for group in range(3):
+                    shift = (group * stride - (0 if side == 0 else 2 * stride)) % LANES
+                    piece = own[half * 3 + group]
+                    piece = pltpu.roll(piece, shift, 1) if shift else piece
+                    total = piece if group == 0 else jnp.where(lanes < group * stride, total, piece)
+                merged.append(total)
+            other = pltpu.roll(merged[1], HALO, 0)
+            keep = rows >= HALO if side == 0 else rows < HALO
+            send_y[side, index] = jnp.where(keep, merged[0], other)
+        return carry
+
+    lax.fori_loop(0, 5 * count_y, pack_y, 0)
+    y_copies = halo("gy", 2, send_y.at[0], send_y.at[1], side_y)
+    for copy in y_copies:
+        copy.wait_recv()
+
+    def unpack_y(index, carry):
+        part, first_x = index // count_y, (index % count_y) * per_y
+        near = [side_y[0, index], pltpu.roll(side_y[0, index], HALO, 0)]
+        far = [side_y[1, index], pltpu.roll(side_y[1, index], HALO, 0)]
+        for half in range(2):
+            for group in range(3):
+                x = first_x + half * 3 + group
+                back = (-group * stride) % LANES
+                ahead = ((2 - group) * stride) % LANES
+                near_piece = pltpu.roll(near[half], back, 1) if back else near[half]
+                far_piece = pltpu.roll(far[half], ahead, 1) if ahead else far[half]
+                plane = out_ref[part, x]
+                plane = jnp.where((rows < HALO) & (lanes < stride), near_piece, plane)
+                plane = jnp.where((rows >= HALO) & (lanes >= 2 * stride), far_piece, plane)
+                out_ref[part, x] = plane
+        return carry
+
+    lax.fori_loop(0, 5 * count_y, unpack_y, 0)
+
+    per_z = 8
+    count_z = planes // per_z
+    column = lax.rem(lanes, stride)
+
+    def pack_z(index, carry):
+        part, first_x = index // count_z, (index % count_z) * per_z
+        own = [out_ref[part, first_x + k] for k in range(per_z)]
+        for side in range(2):
+            begin = HALO if side == 0 else extent_z
+            total = None
+            for k in range(per_z):
+                shift = (k * HALO - begin) % LANES
+                piece = pltpu.roll(own[k], shift, 1) if shift else own[k]
+                total = piece if k == 0 else jnp.where(column < k * HALO, total, piece)
+            send_z[side, index] = total
+        return carry
+
+    lax.fori_loop(0, 5 * count_z, pack_z, 0)
+    z_copies = halo("ba", 3, send_z.at[0], send_z.at[1], side_z)
+    for copy in z_copies:
+        copy.wait_recv()
+
+    def unpack_z(index, carry):
+        part, first_x = index // count_z, (index % count_z) * per_z
+        near, far = side_z[0, index], side_z[1, index]
+        for k in range(per_z):
+            back = (-k * HALO) % LANES
+            ahead = (HALO + extent_z - k * HALO) % LANES
+            near_piece = pltpu.roll(near, back, 1) if back else near
+            far_piece = pltpu.roll(far, ahead, 1) if ahead else far
+            plane = out_ref[part, first_x + k]
+            plane = jnp.where(column < HALO, near_piece, plane)
+            out_ref[part, first_x + k] = jnp.where(
+                column >= HALO + extent_z, far_piece, plane
+            )
+        return carry
+
+    lax.fori_loop(0, 5 * count_z, unpack_z, 0)
+    for copy in moves + x_copies + y_copies + z_copies:
+        copy.wait_send()
+
+
+def gathered(moved, slots, index, kind):
+    extent_x, extent_y, extent_z = kind.shape
+    planes = extent_x + 2 * HALO
+    peers = lax.axis_size("gy")
+    blocks = index.shape[0]
+    layers = HALO * moved.shape[2] // extent_x
+    vmem = pl.BlockSpec(memory_space=pltpu.VMEM)
+    smem = pl.BlockSpec(memory_space=pltpu.SMEM)
+    tile = (SUBLANES, LANES)
+    real = jnp.float32
+    return pl.pallas_call(
+        gather_kernel,
+        out_shape=jax.ShapeDtypeStruct((5, planes) + tile, real),
+        in_specs=[vmem, smem, smem, vmem],
+        out_specs=vmem,
+        scratch_shapes=[
+            pltpu.VMEM((peers,) + moved.shape[1:], real),
+            pltpu.VMEM((peers,) + moved.shape[1:], real),
+            pltpu.VMEM((blocks,) + moved.shape[1:], real),
+            pltpu.VMEM((2, blocks, 4, layers), real),
+            pltpu.VMEM((extent_x, 2) + tile, real),
+            pltpu.VMEM((2, HALO) + tile, real),
+            pltpu.VMEM((2, 5 * planes // 6) + tile, real),
+            pltpu.VMEM((2, 5 * planes // 6) + tile, real),
+            pltpu.VMEM((2, 5 * planes // 8) + tile, real),
+            pltpu.VMEM((2, 5 * planes // 8) + tile, real),
+            pltpu.SemaphoreType.DMA((peers,)),
+            pltpu.SemaphoreType.DMA((peers,)),
+            pltpu.SemaphoreType.DMA((8,)),
+            pltpu.SemaphoreType.DMA((8,)),
+        ],
+        compiler_params=pltpu.CompilerParams(
+            collective_id=0, has_side_effects=True, vmem_limit_bytes=24 * 1024 * 1024
+        ),
+        name="gather",
+    )(moved, slots, index, kind)
+
+
 def on_device(moved_fields, send_slot, recv_index, site_kind):
-    held_blocks = moved_fields[0, 0, 0]
-    wanted = send_slot[0, 0, 0]
-    peer_count = wanted.shape[0]
-    per_peer = wanted.shape[1]
-    flat_wanted = wanted.reshape(peer_count * per_peer)
-    picked = jnp.take(held_blocks, jnp.maximum(flat_wanted, 0), axis=0)
-    picked = jnp.where((flat_wanted >= 0)[:, None, None], picked, 0.0)
-    outgoing = picked.reshape(peer_count, per_peer, held_blocks.shape[1], held_blocks.shape[2])
-    arrived = lax.all_to_all(outgoing, "gy", split_axis=0, concat_axis=0, tiled=True)
-    arrived = arrived.reshape(peer_count * per_peer, held_blocks.shape[1], held_blocks.shape[2])
-    placed = jnp.take(arrived, recv_index[0, 0, 0], axis=0)
-    block_edge = site_kind.shape[0]
-    blocks_here = placed.shape[0]
-    placed = placed.reshape(blocks_here, 4, block_edge, block_edge, block_edge)
-    placed = placed.transpose(1, 2, 3, 0, 4).reshape(
-        4, block_edge, block_edge, blocks_here * block_edge
-    )
-    fields = jnp.concatenate([placed, site_kind[None].astype(jnp.float32)])
-    fields = padded_2(fields, (("gx", 1), ("gy", 2), ("ba", 3)), HALO)
-    parts, extent_x, extent_y, extent_z = fields.shape
-    groups = extent_y // SUBLANES
-    packed = fields.reshape(parts, extent_x, groups, SUBLANES, extent_z)
-    packed = packed.transpose(0, 1, 3, 2, 4).reshape(parts, extent_x, SUBLANES, -1)
-    packed = jnp.pad(packed, ((0, 0), (0, 0), (0, 0), (0, LANES - packed.shape[3])))
-    return lattice(packed, site_kind.shape)
+    fields = gathered(
+        moved_fields[0, 0, 0],
+        send_slot[0, 0, 0].reshape(-1),
+        recv_index[0, 0, 0],
+        site_kind,
+    )
+    return lattice(fields, site_kind.shape)
 
 
 def solution(mesh):

time: 74.3 us -> 54.7 us (0.74)
  Pallas kernels: 15.2 us -> 51.4 us
  waiting for transfers between devices: 23.1 us -> 0 us
  starting transfers between devices: 15.9 us -> 0 us
  local copies, waits for them, and re-layouts: 13.4 us -> 3.16 us
  other arithmetic: 6.14 us -> 0 us
    pallas_call x0 -> x1, Pallas kernels: none -> 36.2 us  [gathered(): pl.pallas_call(gather_kernel, out_shape=jax.ShapeDtypeStruct((5, planes)...]
    ppermute x6 -> x0, waiting for transfers between devices: 15.6 us -> none  [the longest x3 8.09 us: padded_2(): before = lax.ppermute(last, axis, up)]
    ppermute x6 -> x0, starting transfers between devices: 10.5 us -> none  [the longest x3 7.06 us: padded_2(): before = lax.ppermute(last, axis, up)]
    all_to_all x1 -> x0, waiting for transfers between devices: 7.5 us -> none  [on_device(): lax.all_to_all(outgoing, 'gy', split_axis=0, concat_axis=0, tiled=True)]
    all_to_all x1 -> x0, starting transfers between devices: 5.42 us -> none  [on_device(): lax.all_to_all(outgoing, 'gy', split_axis=0, concat_axis=0, tiled=True)]
    slice x3 -> x0, local copies, waits for them, and re-layouts: 5.22 us -> none  [the longest x2 3.73 us: padded_2(): last = lax.slice_in_dim(array, length - width, length, axis=dim)]
    ppermute x2 -> x0, local copies, waits for them, and re-layouts: 4.53 us -> none  [the longest x1 2.82 us: padded_2(): after = lax.ppermute(initial, axis, down)]
    transpose x2 -> x0, other arithmetic: 3.48 us -> none  [the longest x1 2.45 us: on_device(): packed.transpose(0, 1, 3, 2, 4).reshape(parts, extent_x, SUBLANES, -1)]
  transfers between devices with their start and end apart: 7 -> 0, of which waited for: 7 -> 0; matrix products, arithmetic and copies ran while one was open for 4% -> 0% of each run, Pallas kernels for 0% -> 0%
where the time goes in v1:
time: 54.7 us; the launch traced here: 54.5 us
  Pallas kernels  51.4 us (94%)
  local copies, waits for them, and re-layouts  3.16 us (6%)
    pallas_call x1, Pallas kernels, gathered(): pl.pallas_call(gather_kernel, out_shape=jax.ShapeDtypeStruct((5, planes)...  36.2 us
    pallas_call x1, Pallas kernels, lattice(): pl.pallas_call(lattice_kernel, out_shape=jax.ShapeDtypeStruct((19,) + tup...  15.2 us
    unnamed x8, local copies, waits for them, and re-layouts  3.16 us

profile of v1, /device:TPU:1, one launch (start us, length us, event | category | flops | bytes accessed | tf_op | source)
XLA Modules:
  0.0 54.5 jit_solution(8493501998646236702)
XLA Ops:
  0.0 0.0 copy-start
  0.0 0.9 %copy-done = f32[1,1,1,4,4,4096]{5,4,3,2,1,0:T(4,128)S(1)} copy-done((f32[1,1,1,4,4,4096]{5,4,3,2,1,0:T(4,128)S(1)}, f32[1,1,1,4,4,4096]{5,4,3,2,1,0:T(4,128)}, u32[]{:S(2)}) %copy-start) | copy-done | bytes 262168
  1.0 0.0 copy-start.1
  1.0 0.9 %copy-done.1 = s32[16,16,32]{2,1,0:T(8,128)S(1)} copy-done((s32[16,16,32]{2,1,0:T(8,128)S(1)}, s32[16,16,32]{2,1,0:T(8,128)}, u32[]{:S(2)}) %copy-start.1) | copy-done | bytes 32792
  1.9 0.0 copy-start.2
  1.9 0.7 %copy-done.2 = s32[1,1,1,4,1]{3,4,2,1,0:T(1,128)S(1)} copy-done((s32[1,1,1,4,1]{3,4,2,1,0:T(1,128)S(1)}, s32[1,1,1,4,1]{3,4,2,1,0:T(1,128)}, u32[]{:S(2)}) %copy-start.2) | copy-done | bytes 40
  2.5 0.0 copy-start.3
  2.5 0.7 %copy-done.3 = s32[1,1,1,2]{3,2,1,0:T(1,128)S(1)} copy-done((s32[1,1,1,2]{3,2,1,0:T(1,128)S(1)}, s32[1,1,1,2]{3,2,1,0:T(1,128)}, u32[]{:S(2)}) %copy-start.3) | copy-done | bytes 32
  3.2 36.2 %gather.1.fields_ref = f32[5,24,8,128]{3,2,1,0:T(8,128)S(1)} custom-call(f32[4,4,4096]{2,1,0:T(4,128)S(1)} %bitcast.3, s32[4]{0:T(128)S(1)} %bitcast.4, s32[2]{0:T(128)S(1)} %bitcast.5, s32[16,16,32]{2,1,0:T(8,128)S(1)} %copy-done.1), custom_call_target="tpu_custom_call" | custom-call | tf_op jit(solution)/shard_map/gather/pallas_call | solution.py:448
  39.4 15.2 %lattice.1 = f32[19,16,16,32]{3,2,1,0:T(8,128)} custom-call(f32[5,24,8,128]{3,2,1,0:T(8,128)S(1)} %gather.1.fields_ref), custom_call_target="tpu_custom_call" | custom-call | tf_op jit(solution)/shard_map/lattice/pallas_call | solution.py:155
Async XLA Ops:
  0.0 0.9 %copy-start = (f32[1,1,1,4,4,4096]{5,4,3,2,1,0:T(4,128)S(1)}, f32[1,1,1,4,4,4096]{5,4,3,2,1,0:T(4,128)}, u32[]{:S(2)}) copy-start(f32[1,1,1,4,4,4096]{5,4,3,2,1,0:T(4,128)} %param.4) | copy-start | bytes 786436
  1.0 0.9 %copy-start.1 = (s32[16,16,32]{2,1,0:T(8,128)S(1)}, s32[16,16,32]{2,1,0:T(8,128)}, u32[]{:S(2)}) copy-start(s32[16,16,32]{2,1,0:T(8,128)} %kind_ref.1) | copy-start | bytes 98308
  1.9 0.7 %copy-start.2 = (s32[1,1,1,4,1]{3,4,2,1,0:T(1,128)S(1)}, s32[1,1,1,4,1]{3,4,2,1,0:T(1,128)}, u32[]{:S(2)}) copy-start(s32[1,1,1,4,1]{3,4,2,1,0:T(1,128)} %param.5) | copy-start | bytes 52
  2.5 0.7 %copy-start.3 = (s32[1,1,1,2]{3,2,1,0:T(1,128)S(1)}, s32[1,1,1,2]{3,2,1,0:T(1,128)}, u32[]{:S(2)}) copy-start(s32[1,1,1,2]{3,2,1,0:T(1,128)} %param.6) | copy-start | bytes 28

commit v2 on v1

--- a/solution.py
+++ b/solution.py
@@ -52,6 +52,16 @@
     if step_z:
         plane = pltpu.roll(plane, step_z % LANES, 1)
     return plane
+
+
+def unrolled(count, group, body):
+    def step(first, carry):
+        stores = [entry for k in range(group) for entry in body(first * group + k)]
+        for ref, index, value in stores:
+            ref[index] = value
+        return carry
+
+    lax.fori_loop(0, count // group, step, 0)
 
 
 def squared_base(speeds):
@@ -113,29 +123,28 @@
     stride = extent_z + 2 * HALO
     rows = row_ids()
 
-    def begin(x, carry):
+    def begin(x):
         fields = [fields_ref[i, x] for i in range(5)]
-        for i, member in enumerate(start_plane(fields, fields[4])):
-            first[i, x] = member
-        return carry
-
-    lax.fori_loop(0, planes, begin, 0)
+        return [(first, (i, x), m) for i, m in enumerate(start_plane(fields, fields[4]))]
+
+    unrolled(planes, 2, begin)
     source, target = first, second
     for step in range(1, STEPS):
 
-        def advance(x, carry, source=source, target=target):
+        def advance(x, source=source, target=target, step=step):
+            x = x + step
             pulled = [
                 shifted(source[i, x - v[0]], rows, stride, v[1], v[2])
                 for i, v in enumerate(VELOCITIES)
             ]
-            for i, member in enumerate(collide_plane(pulled, fields_ref[4, x])):
-                target[i, x] = member
-            return carry
-
-        lax.fori_loop(step, planes - step, advance, 0)
+            updated = collide_plane(pulled, fields_ref[4, x])
+            return [(target, (i, x), member) for i, member in enumerate(updated)]
+
+        unrolled(planes - 2 * step, 2, advance)
         source, target = target, source
 
-    def finish(x, carry):
+    def finish(x):
+        stores = []
         for i, v in enumerate(VELOCITIES):
             plane = source[i, x + HALO - v[0]]
             offset = HALO - v[1]
@@ -144,10 +153,11 @@
             plane = jnp.where(rows < SUBLANES - offset, plane, crossed)
             for group in range(extent_y // SUBLANES):
                 part = pltpu.roll(plane, LANES - (group * stride + HALO - v[2]), 1)
-                out_ref[i, x, pl.ds(group * SUBLANES, SUBLANES), :] = part[:, :extent_z]
-        return carry
-
-    lax.fori_loop(0, out_ref.shape[1], finish, 0)
+                cut = (i, x, pl.ds(group * SUBLANES, SUBLANES), slice(None))
+                stores.append((out_ref, cut, part[:, :extent_z]))
+        return stores
+
+    unrolled(out_ref.shape[1], 2, finish)
 
 
 def lattice(fields, extents):
@@ -185,11 +195,16 @@
 
 
 def gather_kernel(
+    moved_in,
+    slot_in,
+    index_in,
+    kind_in,
+    out_ref,
     moved_ref,
     slot_ref,
     index_ref,
     kind_ref,
-    out_ref,
+    input_sem,
     staged,
     arrived,
     chosen,
@@ -205,6 +220,19 @@
     halo_sent,
     halo_arrived,
 ):
+    inputs = [
+        pltpu.make_async_copy(source, target, input_sem.at[i])
+        for i, (source, target) in enumerate(
+            (
+                (slot_in, slot_ref),
+                (index_in, index_ref),
+                (moved_in, moved_ref),
+                (kind_in, kind_ref),
+            )
+        )
+    ]
+    for copy in inputs:
+        copy.start()
     extent_x, extent_y, extent_z = kind_ref.shape
     blocks = chosen.shape[0]
     edge = extent_z // blocks
@@ -225,6 +253,8 @@
         pl.semaphore_signal(
             barrier, inc=1, device_id=device, device_id_type=pl.DeviceIdType.MESH
         )
+    for copy in inputs[:3]:
+        copy.wait()
     for offset in range(1, size["gy"]):
         staged[offset] = moved_ref[jnp.maximum(slot_ref[peers[offset]], 0)]
     pl.semaphore_wait(barrier, len(greeted))
@@ -264,7 +294,9 @@
             copy.start()
         return pair
 
-    def lay_kind(x, carry):
+    inputs[3].wait()
+
+    def lay_kind(x):
         parts = []
         for half in range(2):
             kind_wide[x, half, :, pl.ds(0, extent_z)] = kind_ref[
@@ -272,10 +304,10 @@
             ].astype(jnp.float32)
             wide = pltpu.roll(kind_wide[x, half], HALO, 0)
             parts.append(pltpu.roll(wide, HALO, 1))
-        out_ref[4, x + HALO] = grouped(parts[0], parts[1], rows, lanes, stride)
-        return carry
-
-    lax.fori_loop(0, extent_x, lay_kind, 0)
+        plane = grouped(parts[0], parts[1], rows, lanes, stride)
+        return [(out_ref, (4, x + HALO), plane)]
+
+    unrolled(extent_x, 4, lay_kind)
     kind_copies = halo(
         "gx",
         0,
@@ -306,6 +338,7 @@
                 start = pl.multiple_of(x * plane_size + half * LANES, LANES)
                 tiles.append(read(block, pl.ds(start, LANES)))
         quarter, half_lanes, whole = LANES // 4, LANES // 2, LANES
+        stores = []
         for part in range(4):
             picked = []
             for source, tile in enumerate(tiles):
@@ -326,13 +359,14 @@
             far = pltpu.roll(joined, (HALO + edge - quarter) % whole, 1)
             low = jnp.where((lanes & (half_lanes - 1)) < HALO + edge, near, far)
             high = pltpu.roll(low, half_lanes, 1)
-            out_ref[part, target_x] = grouped(low, high, rows, lanes, stride)
-
-    def lay_own(x, carry):
-        lay_fields(lambda block, cut: chosen[block, :, cut], x, x + HALO)
-        return carry
-
-    lax.fori_loop(0, extent_x, lay_own, 0)
+            plane = grouped(low, high, rows, lanes, stride)
+            stores.append((out_ref, (part, target_x), plane))
+        return stores
+
+    def lay_own(x):
+        return lay_fields(lambda block, cut: chosen[block, :, cut], x, x + HALO)
+
+    unrolled(extent_x, 4, lay_own)
     for copy in kind_copies:
         copy.wait()
     for copy in x_copies:
@@ -341,17 +375,19 @@
     for side in range(2):
         first_x = side * (extent_x + HALO)
 
-        def lay_side(x, carry, side=side, first_x=first_x):
-            lay_fields(lambda block, cut: side_x[side, block, :, cut], x, first_x + x)
-            out_ref[4, first_x + x] = kind_x[side, x]
-            return carry
-
-        lax.fori_loop(0, HALO, lay_side, 0)
+        def lay_side(x, side=side, first_x=first_x):
+            stores = lay_fields(
+                lambda block, cut: side_x[side, block, :, cut], x, first_x + x
+            )
+            return stores + [(out_ref, (4, first_x + x), kind_x[side, x])]
+
+        unrolled(HALO, 4, lay_side)
 
     per_y = 6
     count_y = planes // per_y
 
-    def pack_y(index, carry):
+    def pack_y(index):
+        stores = []
         part, first_x = index // count_y, (index % count_y) * per_y
         own = [out_ref[part, first_x + k] for k in range(per_y)]
         for side in range(2):
@@ -366,15 +402,16 @@
                 merged.append(total)
             other = pltpu.roll(merged[1], HALO, 0)
             keep = rows >= HALO if side == 0 else rows < HALO
-            send_y[side, index] = jnp.where(keep, merged[0], other)
-        return carry
-
-    lax.fori_loop(0, 5 * count_y, pack_y, 0)
+            stores.append((send_y, (side, index), jnp.where(keep, merged[0], other)))
+        return stores
+
+    unrolled(5 * count_y, 4, pack_y)
     y_copies = halo("gy", 2, send_y.at[0], send_y.at[1], side_y)
     for copy in y_copies:
         copy.wait_recv()
 
-    def unpack_y(index, carry):
+    def unpack_y(index):
+        stores = []
         part, first_x = index // count_y, (index % count_y) * per_y
         near = [side_y[0, index], pltpu.roll(side_y[0, index], HALO, 0)]
         far = [side_y[1, index], pltpu.roll(side_y[1, index], HALO, 0)]
@@ -388,16 +425,17 @@
                 plane = out_ref[part, x]
                 plane = jnp.where((rows < HALO) & (lanes < stride), near_piece, plane)
                 plane = jnp.where((rows >= HALO) & (lanes >= 2 * stride), far_piece, plane)
-                out_ref[part, x] = plane
-        return carry
-
-    lax.fori_loop(0, 5 * count_y, unpack_y, 0)
+                stores.append((out_ref, (part, x), plane))
+        return stores
+
+    unrolled(5 * count_y, 4, unpack_y)
 
     per_z = 8
     count_z = planes // per_z
     column = lax.rem(lanes, stride)
 
-    def pack_z(index, carry):
+    def pack_z(index):
+        stores = []
         part, first_x = index // count_z, (index % count_z) * per_z
         own = [out_ref[part, first_x + k] for k in range(per_z)]
         for side in range(2):
@@ -407,15 +445,16 @@
                 shift = (k * HALO - begin) % LANES
                 piece = pltpu.roll(own[k], shift, 1) if shift else own[k]
                 total = piece if k == 0 else jnp.where(column < k * HALO, total, piece)
-            send_z[side, index] = total
-        return carry
-
-    lax.fori_loop(0, 5 * count_z, pack_z, 0)
+            stores.append((send_z, (side, index), total))
+        return stores
+
+    unrolled(5 * count_z, 3, pack_z)
     z_copies = halo("ba", 3, send_z.at[0], send_z.at[1], side_z)
     for copy in z_copies:
         copy.wait_recv()
 
-    def unpack_z(index, carry):
+    def unpack_z(index):
+        stores = []
         part, first_x = index // count_z, (index % count_z) * per_z
         near, far = side_z[0, index], side_z[1, index]
         for k in range(per_z):
@@ -425,12 +464,11 @@
             far_piece = pltpu.roll(far, ahead, 1) if ahead else far
             plane = out_ref[part, first_x + k]
             plane = jnp.where(column < HALO, near_piece, plane)
-            out_ref[part, first_x + k] = jnp.where(
-                column >= HALO + extent_z, far_piece, plane
-            )
-        return carry
-
-    lax.fori_loop(0, 5 * count_z, unpack_z, 0)
+            plane = jnp.where(column >= HALO + extent_z, far_piece, plane)
+            stores.append((out_ref, (part, first_x + k), plane))
+        return stores
+
+    unrolled(5 * count_z, 3, unpack_z)
     for copy in moves + x_copies + y_copies + z_copies:
         copy.wait_send()
 
@@ -442,15 +480,20 @@
     blocks = index.shape[0]
     layers = HALO * moved.shape[2] // extent_x
     vmem = pl.BlockSpec(memory_space=pltpu.VMEM)
-    smem = pl.BlockSpec(memory_space=pltpu.SMEM)
+    anywhere = pl.BlockSpec(memory_space=pltpu.HBM)
     tile = (SUBLANES, LANES)
     real = jnp.float32
     return pl.pallas_call(
         gather_kernel,
         out_shape=jax.ShapeDtypeStruct((5, planes) + tile, real),
-        in_specs=[vmem, smem, smem, vmem],
+        in_specs=[anywhere] * 4,
         out_specs=vmem,
         scratch_shapes=[
+            pltpu.VMEM(moved.shape, real),
+            pltpu.SMEM(slots.shape, jnp.int32),
+            pltpu.SMEM(index.shape, jnp.int32),
+            pltpu.VMEM(kind.shape, jnp.int32),
+            pltpu.SemaphoreType.DMA((4,)),
             pltpu.VMEM((peers,) + moved.shape[1:], real),
             pltpu.VMEM((peers,) + moved.shape[1:], real),
             pltpu.VMEM((blocks,) + moved.shape[1:], real),
@@ -467,7 +510,7 @@
             pltpu.SemaphoreType.DMA((8,)),
         ],
         compiler_params=pltpu.CompilerParams(
-            collective_id=0, has_side_effects=True, vmem_limit_bytes=24 * 1024 * 1024
+            collective_id=0, has_side_effects=True, vmem_limit_bytes=60 * 1024 * 1024
         ),
         name="gather",
     )(moved, slots, index, kind)

time: 54.7 us -> 38.2 us (0.70)
  Pallas kernels: 51.4 us -> 37 us
  local copies, waits for them, and re-layouts: 3.16 us -> 1.02 us
    pallas_call x1, Pallas kernels: 36.2 us -> 27.6 us  [gathered(): pl.pallas_call(gather_kernel, out_shape=jax.ShapeDtypeStruct((5, planes)...]
    pallas_call x1, Pallas kernels: 15.2 us -> 9.39 us  [lattice(): pl.pallas_call(lattice_kernel, out_shape=jax.ShapeDtypeStruct((19,) + tup...]
    unnamed x8 -> x2, local copies, waits for them, and re-layouts: 3.16 us -> 1.02 us
where the time goes in v2:
time: 38.2 us; the launch traced here: 38 us
  Pallas kernels  37 us (97%)
  local copies, waits for them, and re-layouts  1.02 us (3%)
    pallas_call x1, Pallas kernels, gathered(): pl.pallas_call(gather_kernel, out_shape=jax.ShapeDtypeStruct((5, planes)...  27.6 us
    pallas_call x1, Pallas kernels, lattice(): pl.pallas_call(lattice_kernel, out_shape=jax.ShapeDtypeStruct((19,) + tup...  9.39 us
    unnamed x2, local copies, waits for them, and re-layouts  1.02 us

profile of v2, /device:TPU:1, one launch (start us, length us, event | category | flops | bytes accessed | tf_op | source)
XLA Modules:
  0.0 38.0 jit_solution(8063080470885052606)
XLA Ops:
  0.0 27.6 %gather.1.fields_ref = f32[5,24,8,128]{3,2,1,0:T(8,128)} custom-call(f32[4,4,4096]{2,1,0:T(4,128)} %bitcast.3, s32[4]{0:T(128)} %bitcast.4, s32[2]{0:T(128)} %bitcast.5, s32[16,16,32]{2,1,0:T(8,128)} %kind_in.1), custom_call_target="tpu_custom_call" | custom-call | tf_op jit(solution)/shard_map/gather/pallas_call | solution.py:486
  27.6 0.0 copy-start
  27.6 1.0 %copy-done = f32[5,24,8,128]{3,2,1,0:T(8,128)S(1)} copy-done((f32[5,24,8,128]{3,2,1,0:T(8,128)S(1)}, f32[5,24,8,128]{3,2,1,0:T(8,128)}, u32[]{:S(2)}) %copy-start) | copy-done | bytes 491544
  28.6 9.4 %lattice.1 = f32[19,16,16,32]{3,2,1,0:T(8,128)} custom-call(f32[5,24,8,128]{3,2,1,0:T(8,128)S(1)} %copy-done), custom_call_target="tpu_custom_call" | custom-call | tf_op jit(solution)/shard_map/lattice/pallas_call | solution.py:165
Async XLA Ops:
  27.6 1.0 %copy-start = (f32[5,24,8,128]{3,2,1,0:T(8,128)S(1)}, f32[5,24,8,128]{3,2,1,0:T(8,128)}, u32[]{:S(2)}) copy-start(f32[5,24,8,128]{3,2,1,0:T(8,128)} %gather.1.fields_ref) | copy-start | bytes 1474564

commit v3 on v2

--- a/solution.py
+++ b/solution.py
@@ -117,17 +117,30 @@
     return result
 
 
-def lattice_kernel(fields_ref, out_ref, first, second):
+def lattice_kernel(fields_in, out, fields_ref, result, first, second, in_sem, out_sem):
     planes = fields_ref.shape[1]
-    extent_y, extent_z = out_ref.shape[2:]
+    extent_x, extent_y, extent_z = out.shape[1:]
+    count = in_sem.shape[0]
+    cuts = [pl.ds(i * (planes // count), planes // count) for i in range(count)]
+    loads = [
+        pltpu.make_async_copy(fields_in.at[:, cut], fields_ref.at[:, cut], in_sem.at[i])
+        for i, cut in enumerate(cuts)
+    ]
+    for load in loads:
+        load.start()
     stride = extent_z + 2 * HALO
     rows = row_ids()
 
-    def begin(x):
+    def begin(x, offset):
+        x = x + offset
         fields = [fields_ref[i, x] for i in range(5)]
         return [(first, (i, x), m) for i, m in enumerate(start_plane(fields, fields[4]))]
 
-    unrolled(planes, 2, begin)
+    for i, load in enumerate(loads):
+        load.wait()
+        unrolled(
+            planes // count, 2, functools.partial(begin, offset=i * (planes // count))
+        )
     source, target = first, second
     for step in range(1, STEPS):
 
@@ -143,7 +156,8 @@
         unrolled(planes - 2 * step, 2, advance)
         source, target = target, source
 
-    def finish(x):
+    def finish(x, offset):
+        x = x + offset
         stores = []
         for i, v in enumerate(VELOCITIES):
             plane = source[i, x + HALO - v[0]]
@@ -154,10 +168,21 @@
             for group in range(extent_y // SUBLANES):
                 part = pltpu.roll(plane, LANES - (group * stride + HALO - v[2]), 1)
                 cut = (i, x, pl.ds(group * SUBLANES, SUBLANES), slice(None))
-                stores.append((out_ref, cut, part[:, :extent_z]))
+                stores.append((result, cut, part[:, :extent_z]))
         return stores
 
-    unrolled(out_ref.shape[1], 2, finish)
+    count = out_sem.shape[0]
+    saves = []
+    for i in range(count):
+        length = extent_x // count
+        unrolled(length, 2, functools.partial(finish, offset=i * length))
+        cut = pl.ds(i * length, length)
+        saves.append(
+            pltpu.make_async_copy(result.at[:, cut], out.at[:, cut], out_sem.at[i])
+        )
+        saves[-1].start()
+    for save in saves:
+        save.wait()
 
 
 def lattice(fields, extents):
@@ -165,10 +190,17 @@
     return pl.pallas_call(
         lattice_kernel,
         out_shape=jax.ShapeDtypeStruct((19,) + tuple(extents), jnp.float32),
-        in_specs=[pl.BlockSpec(memory_space=pltpu.VMEM)],
-        out_specs=pl.BlockSpec(memory_space=pltpu.VMEM),
-        scratch_shapes=[pltpu.VMEM((19, planes, SUBLANES, LANES), jnp.float32)] * 2,
-        compiler_params=pltpu.CompilerParams(vmem_limit_bytes=24 * 1024 * 1024),
+        in_specs=[pl.BlockSpec(memory_space=pltpu.HBM)],
+        out_specs=pl.BlockSpec(memory_space=pltpu.HBM),
+        scratch_shapes=[
+            pltpu.VMEM(fields.shape, jnp.float32),
+            pltpu.VMEM((19,) + tuple(extents), jnp.float32),
+            pltpu.VMEM((19, planes, SUBLANES, LANES), jnp.float32),
+            pltpu.VMEM((19, planes, SUBLANES, LANES), jnp.float32),
+            pltpu.SemaphoreType.DMA((4,)),
+            pltpu.SemaphoreType.DMA((4,)),
+        ],
+        compiler_params=pltpu.CompilerParams(vmem_limit_bytes=60 * 1024 * 1024),
         name="lattice",
     )(fields)
 
@@ -212,7 +244,7 @@
     kind_wide,
     kind_x,
     send_y,
-    side_y,
+    recv_y,
     send_z,
     side_z,
     sent_sem,
@@ -249,6 +281,12 @@
     barrier = pltpu.get_barrier_semaphore()
     greeted = [mesh_device(gy=peer) for peer in peers[1:]]
     greeted += [up["gx"], down["gx"], up["ba"], down["ba"]]
+    ahead_x, ahead_y = (lax.rem(me[a] + 1, size[a]) for a in ("gx", "gy"))
+    behind_x, behind_y = (lax.rem(me[a] + size[a] - 1, size[a]) for a in ("gx", "gy"))
+    corners = [
+        [mesh_device(gx=x, gy=y) for x in (behind_x, ahead_x)] for y in (behind_y, ahead_y)
+    ]
+    greeted += corners[0] + corners[1]
     for device in greeted:
         pl.semaphore_signal(
             barrier, inc=1, device_id=device, device_id_type=pl.DeviceIdType.MESH
@@ -294,6 +332,69 @@
             copy.start()
         return pair
 
+    quad_lanes = LANES // HALO
+    quads = extent_x // HALO
+
+    def pack_y(pair, quad):
+        stores = []
+        for side in range(2):
+            merged = []
+            for half in range(2):
+                part = min(2 * pair + half, 4)
+                total = None
+                for k in range(HALO):
+                    begin = HALO + (0 if side == 0 else 2 * stride)
+                    piece = out_ref[part, quad * HALO + HALO + k]
+                    piece = pltpu.roll(piece, (k * quad_lanes - begin) % LANES, 1)
+                    total = piece if k == 0 else jnp.where(lanes < k * quad_lanes, total, piece)
+                merged.append(total)
+            other = pltpu.roll(merged[1], HALO, 0)
+            keep = rows >= HALO if side == 0 else rows < HALO
+            stores.append((send_y, (side, quad, pair), jnp.where(keep, merged[0], other)))
+        return stores
+
+    def unpack_y(pair, quad):
+        stores = []
+        near, far = recv_y[0, quad, pair], recv_y[1, quad, pair]
+        for half in range(1 if pair == 2 else 2):
+            part = 2 * pair + half
+            if half:
+                near, far = pltpu.roll(near, HALO, 0), pltpu.roll(far, HALO, 0)
+            for k in range(HALO):
+                x = quad * HALO + k
+                near_piece = pltpu.roll(near, (HALO - k * quad_lanes) % LANES, 1)
+                far_piece = pltpu.roll(
+                    far, (HALO + 2 * stride - k * quad_lanes) % LANES, 1
+                )
+                plane = out_ref[part, x]
+                plane = jnp.where((rows < HALO) & (lanes < stride), near_piece, plane)
+                plane = jnp.where((rows >= HALO) & (lanes >= 2 * stride), far_piece, plane)
+                stores.append((out_ref, (part, x), plane))
+        return stores
+
+    def halo_y(first, pairs):
+        copies = []
+        for toward in range(2):
+            send, land = toward, 1 - toward
+            routes = (
+                ((up if toward else down)["gy"], pl.ds(0, quads), pl.ds(1, quads)),
+                (corners[toward][1], pl.ds(quads - 1, 1), pl.ds(0, 1)),
+                (corners[toward][0], pl.ds(0, 1), pl.ds(quads + 1, 1)),
+            )
+            for number, (device, source, target) in enumerate(routes):
+                sem = first + toward * 3 + number
+                copies.append(
+                    remote(
+                        send_y.at[send, source, pairs],
+                        recv_y.at[land, target, pairs],
+                        halo_sent.at[sem],
+                        halo_arrived.at[sem],
+                        device,
+                    )
+                )
+                copies[-1].start()
+        return copies
+
     inputs[3].wait()
 
     def lay_kind(x):
@@ -315,6 +416,8 @@
         out_ref.at[4, pl.ds(extent_x, HALO)],
         kind_x,
     )
+    unrolled(quads, 4, lambda quad: pack_y(2, quad))
+    kind_y = halo_y(12, pl.ds(2, 1))
 
     for move in moves:
         move.wait_recv()
@@ -367,6 +470,9 @@
         return lay_fields(lambda block, cut: chosen[block, :, cut], x, x + HALO)
 
     unrolled(extent_x, 4, lay_own)
+    for pair in range(2):
+        unrolled(quads, 4, lambda quad, pair=pair: pack_y(pair, quad))
+    y_copies = halo_y(6, pl.ds(0, 2))
     for copy in kind_copies:
         copy.wait()
     for copy in x_copies:
@@ -383,52 +489,10 @@
 
         unrolled(HALO, 4, lay_side)
 
-    per_y = 6
-    count_y = planes // per_y
-
-    def pack_y(index):
-        stores = []
-        part, first_x = index // count_y, (index % count_y) * per_y
-        own = [out_ref[part, first_x + k] for k in range(per_y)]
-        for side in range(2):
-            merged = []
-            for half in range(2):
-                total = None
-                for group in range(3):
-                    shift = (group * stride - (0 if side == 0 else 2 * stride)) % LANES
-                    piece = own[half * 3 + group]
-                    piece = pltpu.roll(piece, shift, 1) if shift else piece
-                    total = piece if group == 0 else jnp.where(lanes < group * stride, total, piece)
-                merged.append(total)
-            other = pltpu.roll(merged[1], HALO, 0)
-            keep = rows >= HALO if side == 0 else rows < HALO
-            stores.append((send_y, (side, index), jnp.where(keep, merged[0], other)))
-        return stores
-
-    unrolled(5 * count_y, 4, pack_y)
-    y_copies = halo("gy", 2, send_y.at[0], send_y.at[1], side_y)
-    for copy in y_copies:
+    for copy in y_copies + kind_y:
         copy.wait_recv()
-
-    def unpack_y(index):
-        stores = []
-        part, first_x = index // count_y, (index % count_y) * per_y
-        near = [side_y[0, index], pltpu.roll(side_y[0, index], HALO, 0)]
-        far = [side_y[1, index], pltpu.roll(side_y[1, index], HALO, 0)]
-        for half in range(2):
-            for group in range(3):
-                x = first_x + half * 3 + group
-                back = (-group * stride) % LANES
-                ahead = ((2 - group) * stride) % LANES
-                near_piece = pltpu.roll(near[half], back, 1) if back else near[half]
-                far_piece = pltpu.roll(far[half], ahead, 1) if ahead else far[half]
-                plane = out_ref[part, x]
-                plane = jnp.where((rows < HALO) & (lanes < stride), near_piece, plane)
-                plane = jnp.where((rows >= HALO) & (lanes >= 2 * stride), far_piece, plane)
-                stores.append((out_ref, (part, x), plane))
-        return stores
-
-    unrolled(5 * count_y, 4, unpack_y)
+    for pair in range(3):
+        unrolled(quads + 2, 3, lambda quad, pair=pair: unpack_y(pair, quad))
 
     per_z = 8
     count_z = planes // per_z
@@ -449,7 +513,7 @@
         return stores
 
     unrolled(5 * count_z, 3, pack_z)
-    z_copies = halo("ba", 3, send_z.at[0], send_z.at[1], side_z)
+    z_copies = halo("ba", 2, send_z.at[0], send_z.at[1], side_z)
     for copy in z_copies:
         copy.wait_recv()
 
@@ -469,7 +533,7 @@
         return stores
 
     unrolled(5 * count_z, 3, unpack_z)
-    for copy in moves + x_copies + y_copies + z_copies:
+    for copy in moves + x_copies + y_copies + kind_y + z_copies:
         copy.wait_send()
 
 
@@ -500,14 +564,14 @@
             pltpu.VMEM((2, blocks, 4, layers), real),
             pltpu.VMEM((extent_x, 2) + tile, real),
             pltpu.VMEM((2, HALO) + tile, real),
-            pltpu.VMEM((2, 5 * planes // 6) + tile, real),
-            pltpu.VMEM((2, 5 * planes // 6) + tile, real),
+            pltpu.VMEM((2, extent_x // HALO, 3) + tile, real),
+            pltpu.VMEM((2, extent_x // HALO + 2, 3) + tile, real),
             pltpu.VMEM((2, 5 * planes // 8) + tile, real),
             pltpu.VMEM((2, 5 * planes // 8) + tile, real),
             pltpu.SemaphoreType.DMA((peers,)),
             pltpu.SemaphoreType.DMA((peers,)),
-            pltpu.SemaphoreType.DMA((8,)),
-            pltpu.SemaphoreType.DMA((8,)),
+            pltpu.SemaphoreType.DMA((18,)),
+            pltpu.SemaphoreType.DMA((18,)),
         ],
         compiler_params=pltpu.CompilerParams(
             collective_id=0, has_side_effects=True, vmem_limit_bytes=60 * 1024 * 1024

time: 38.2 us -> 36.5 us (0.955)
  local copies, waits for them, and re-layouts: 1.02 us -> 0 us
  Pallas kernels: 37 us -> 36.3 us
    unnamed x2 -> x0, local copies, waits for them, and re-layouts: 1.02 us -> none
    pallas_call x1, Pallas kernels: 27.6 us -> 26.6 us  [gathered(): pl.pallas_call(gather_kernel, out_shape=jax.ShapeDtypeStruct((5, planes)...]
where the time goes in v3:
time: 36.5 us; the launch traced here: 36.3 us
  Pallas kernels  36.3 us (99%)
    pallas_call x1, Pallas kernels, gathered(): pl.pallas_call(gather_kernel, out_shape=jax.ShapeDtypeStruct((5, planes)...  26.6 us
    pallas_call x1, Pallas kernels, lattice(): pl.pallas_call(lattice_kernel, out_shape=jax.ShapeDtypeStruct((19,) + tup...  9.73 us

profile of v3, /device:TPU:1, one launch (start us, length us, event | category | flops | bytes accessed | tf_op | source)
XLA Modules:
  0.0 36.3 jit_solution(14573754888304984571)
XLA Ops:
  0.0 26.6 %gather.1.fields_in = f32[5,24,8,128]{3,2,1,0:T(8,128)} custom-call(f32[4,4,4096]{2,1,0:T(4,128)} %bitcast.3, s32[4]{0:T(128)} %bitcast.4, s32[2]{0:T(128)} %bitcast.5, s32[16,16,32]{2,1,0:T(8,128)} %kind_in.1), custom_call_target="tpu_custom_call" | custom-call | tf_op jit(solution)/shard_map/gather/pallas_call | solution.py:550
  26.6 9.7 %lattice.1 = f32[19,16,16,32]{3,2,1,0:T(8,128)} custom-call(f32[5,24,8,128]{3,2,1,0:T(8,128)} %gather.1.fields_in), custom_call_target="tpu_custom_call" | custom-call | tf_op jit(solution)/shard_map/lattice/pallas_call | solution.py:190

commit v4 on v3

--- a/solution.py
+++ b/solution.py
@@ -55,13 +55,22 @@
 
 
 def unrolled(count, group, body):
-    def step(first, carry):
-        stores = [entry for k in range(group) for entry in body(first * group + k)]
+    def several(sites):
+        stores = [entry for site in sites for entry in body(site)]
         for ref, index, value in stores:
             ref[index] = value
+
+    def step(first, carry):
+        several([first * group + k for k in range(group)])
         return carry
 
-    lax.fori_loop(0, count // group, step, 0)
+    whole = count // group
+    if whole > 1:
+        lax.fori_loop(0, whole, step, 0)
+    elif whole:
+        several(range(group))
+    if count % group:
+        several(range(whole * group, count))
 
 
 def squared_base(speeds):
@@ -139,7 +148,7 @@
     for i, load in enumerate(loads):
         load.wait()
         unrolled(
-            planes // count, 2, functools.partial(begin, offset=i * (planes // count))
+            planes // count, 3, functools.partial(begin, offset=i * (planes // count))
         )
     source, target = first, second
     for step in range(1, STEPS):
@@ -153,7 +162,7 @@
             updated = collide_plane(pulled, fields_ref[4, x])
             return [(target, (i, x), member) for i, member in enumerate(updated)]
 
-        unrolled(planes - 2 * step, 2, advance)
+        unrolled(planes - 2 * step, 4, advance)
         source, target = target, source
 
     def finish(x, offset):
@@ -175,7 +184,7 @@
     saves = []
     for i in range(count):
         length = extent_x // count
-        unrolled(length, 2, functools.partial(finish, offset=i * length))
+        unrolled(length, 4, functools.partial(finish, offset=i * length))
         cut = pl.ds(i * length, length)
         saves.append(
             pltpu.make_async_copy(result.at[:, cut], out.at[:, cut], out_sem.at[i])
@@ -238,8 +247,12 @@
     kind_ref,
     input_sem,
     staged,
-    arrived,
-    chosen,
+    arrived_low,
+    arrived_high,
+    arrived_mid,
+    chosen_low,
+    chosen_high,
+    chosen_mid,
     side_x,
     kind_wide,
     kind_x,
@@ -266,7 +279,7 @@
     for copy in inputs:
         copy.start()
     extent_x, extent_y, extent_z = kind_ref.shape
-    blocks = chosen.shape[0]
+    blocks = chosen_low.shape[0]
     edge = extent_z // blocks
     stride = extent_z + 2 * HALO
     planes = extent_x + 2 * HALO
@@ -297,19 +310,29 @@
         staged[offset] = moved_ref[jnp.maximum(slot_ref[peers[offset]], 0)]
     pl.semaphore_wait(barrier, len(greeted))
 
+    plane_size = moved_ref.shape[2] // extent_x
+    layers = HALO * plane_size
+    pieces = (
+        (arrived_low, 0, layers),
+        (arrived_high, extent_x * plane_size - layers, layers),
+        (arrived_mid, layers, extent_x * plane_size - 2 * layers),
+    )
     moves = []
-    for offset in range(1, size["gy"]):
-        moves.append(
-            remote(
-                staged.at[offset],
-                arrived.at[me["gy"]],
-                sent_sem.at[offset],
-                arrived_sem.at[offset],
+    for number, (target, begin, length) in enumerate(pieces):
+        moves.append([])
+        for offset in range(1, size["gy"]):
+            copy = remote(
+                staged.at[offset, :, pl.ds(begin, length)],
+                target.at[me["gy"]],
+                sent_sem.at[number, offset],
+                arrived_sem.at[number, offset],
                 mesh_device(gy=peers[offset]),
             )
-        )
-        moves[-1].start()
-    arrived[me["gy"]] = moved_ref[jnp.maximum(slot_ref[me["gy"]], 0)]
+            copy.start()
+            moves[-1].append(copy)
+    own_slot = jnp.maximum(slot_ref[me["gy"]], 0)
+    for target, begin, length in pieces:
+        target[me["gy"]] = moved_ref[own_slot, :, pl.ds(begin, length)]
 
     def halo(axis, number, low_source, high_source, target):
         pair = [
@@ -372,24 +395,33 @@
                 stores.append((out_ref, (part, x), plane))
         return stores
 
-    def halo_y(first, pairs):
+    last = quads - 1
+    outer_y = (
+        ("straight", 0, 1, 1),
+        ("straight", last, 1, last + 1),
+        ("ahead", last, 1, 0),
+        ("behind", 0, 1, quads + 1),
+    )
+    inner_y = (("straight", 1, quads - 2, 2),)
+    whole_y = (("straight", 0, quads, 1),) + outer_y[2:]
+
+    def halo_y(first, pairs, routes):
         copies = []
         for toward in range(2):
-            send, land = toward, 1 - toward
-            routes = (
-                ((up if toward else down)["gy"], pl.ds(0, quads), pl.ds(1, quads)),
-                (corners[toward][1], pl.ds(quads - 1, 1), pl.ds(0, 1)),
-                (corners[toward][0], pl.ds(0, 1), pl.ds(quads + 1, 1)),
-            )
-            for number, (device, source, target) in enumerate(routes):
-                sem = first + toward * 3 + number
+            devices = {
+                "straight": (up if toward else down)["gy"],
+                "behind": corners[toward][0],
+                "ahead": corners[toward][1],
+            }
+            for route, source, length, target in routes:
+                sem = first + len(copies)
                 copies.append(
                     remote(
-                        send_y.at[send, source, pairs],
-                        recv_y.at[land, target, pairs],
+                        send_y.at[toward, pl.ds(source, length), pairs],
+                        recv_y.at[1 - toward, pl.ds(target, length), pairs],
                         halo_sent.at[sem],
                         halo_arrived.at[sem],
-                        device,
+                        devices[route],
                     )
                 )
                 copies[-1].start()
@@ -417,22 +449,13 @@
         kind_x,
     )
     unrolled(quads, 4, lambda quad: pack_y(2, quad))
-    kind_y = halo_y(12, pl.ds(2, 1))
-
-    for move in moves:
-        move.wait_recv()
-    for block in range(blocks):
-        chosen[block] = arrived[index_ref[block]]
-
-    plane_size = edge * edge
-    layers = HALO * plane_size
-    x_copies = halo(
-        "gx",
-        1,
-        chosen.at[:, :, pl.ds(0, layers)],
-        chosen.at[:, :, pl.ds(extent_x * plane_size - layers, layers)],
-        side_x,
-    )
+    kind_y = halo_y(18, pl.ds(2, 1), whole_y)
+
+    def choose(number, target):
+        for copy in moves[number]:
+            copy.wait_recv()
+        for block in range(blocks):
+            target[block] = pieces[number][0][index_ref[block]]
 
     def lay_fields(read, x, target_x):
         tiles = []
@@ -466,13 +489,20 @@
             stores.append((out_ref, (part, target_x), plane))
         return stores
 
-    def lay_own(x):
-        return lay_fields(lambda block, cut: chosen[block, :, cut], x, x + HALO)
-
-    unrolled(extent_x, 4, lay_own)
+    def lay_own(source, count, first_x):
+        def lay(x):
+            return lay_fields(lambda block, cut: source[block, :, cut], x, first_x + x)
+
+        unrolled(count, 4, lay)
+
+    choose(0, chosen_low)
+    choose(1, chosen_high)
+    x_copies = halo("gx", 1, chosen_low, chosen_high, side_x)
+    lay_own(chosen_low, HALO, HALO)
+    lay_own(chosen_high, HALO, extent_x)
     for pair in range(2):
-        unrolled(quads, 4, lambda quad, pair=pair: pack_y(pair, quad))
-    y_copies = halo_y(6, pl.ds(0, 2))
+        unrolled(2, 2, lambda k, pair=pair: pack_y(pair, k * last))
+    outer_copies = halo_y(8, pl.ds(0, 2), outer_y)
     for copy in kind_copies:
         copy.wait()
     for copy in x_copies:
@@ -489,18 +519,19 @@
 
         unrolled(HALO, 4, lay_side)
 
-    for copy in y_copies + kind_y:
-        copy.wait_recv()
-    for pair in range(3):
-        unrolled(quads + 2, 3, lambda quad, pair=pair: unpack_y(pair, quad))
+    choose(2, chosen_mid)
+    lay_own(chosen_mid, extent_x - 2 * HALO, 2 * HALO)
+    for pair in range(2):
+        unrolled(quads - 2, 2, lambda k, pair=pair: pack_y(pair, 1 + k))
+    inner_copies = halo_y(16, pl.ds(0, 2), inner_y)
 
     per_z = 8
     count_z = planes // per_z
     column = lax.rem(lanes, stride)
 
-    def pack_z(index):
+    def pack_z(part, slot):
         stores = []
-        part, first_x = index // count_z, (index % count_z) * per_z
+        first_x = group_z[slot] * per_z
         own = [out_ref[part, first_x + k] for k in range(per_z)]
         for side in range(2):
             begin = HALO if side == 0 else extent_z
@@ -509,18 +540,13 @@
                 shift = (k * HALO - begin) % LANES
                 piece = pltpu.roll(own[k], shift, 1) if shift else own[k]
                 total = piece if k == 0 else jnp.where(column < k * HALO, total, piece)
-            stores.append((send_z, (side, index), total))
+            stores.append((send_z, (side, slot, part), total))
         return stores
 
-    unrolled(5 * count_z, 3, pack_z)
-    z_copies = halo("ba", 2, send_z.at[0], send_z.at[1], side_z)
-    for copy in z_copies:
-        copy.wait_recv()
-
-    def unpack_z(index):
+    def unpack_z(part, slot):
         stores = []
-        part, first_x = index // count_z, (index % count_z) * per_z
-        near, far = side_z[0, index], side_z[1, index]
+        first_x = group_z[slot] * per_z
+        near, far = side_z[0, slot, part], side_z[1, slot, part]
         for k in range(per_z):
             back = (-k * HALO) % LANES
             ahead = (HALO + extent_z - k * HALO) % LANES
@@ -532,8 +558,31 @@
             stores.append((out_ref, (part, first_x + k), plane))
         return stores
 
-    unrolled(5 * count_z, 3, unpack_z)
-    for copy in moves + x_copies + y_copies + kind_y + z_copies:
+    def exchange_z(number, slots):
+        for slot in slots:
+            unrolled(5, 5, lambda part, slot=slot: pack_z(part, slot))
+        cut = pl.ds(slots[0], len(slots))
+        return halo("ba", number, send_z.at[0, cut], send_z.at[1, cut], side_z.at[:, cut])
+
+    group_z = [0] + [count_z - 1] + list(range(1, count_z - 1))
+    for copy in outer_copies + kind_y:
+        copy.wait_recv()
+    for pair in range(3):
+        unrolled(2, 2, lambda k, pair=pair: unpack_y(pair, k))
+        unrolled(2, 2, lambda k, pair=pair: unpack_y(pair, quads + k))
+    outer_z = exchange_z(2, [0, 1])
+    for copy in inner_copies:
+        copy.wait_recv()
+    for pair in range(3):
+        unrolled(2, 2, lambda k, pair=pair: unpack_y(pair, 2 + k))
+    inner_z = exchange_z(3, list(range(2, count_z)))
+    for copies, slots in ((outer_z, [0, 1]), (inner_z, list(range(2, count_z)))):
+        for copy in copies:
+            copy.wait_recv()
+        for slot in slots:
+            unrolled(5, 5, lambda part, slot=slot: unpack_z(part, slot))
+    sent = moves[0] + moves[1] + moves[2] + x_copies + kind_y
+    for copy in sent + outer_copies + inner_copies + outer_z + inner_z:
         copy.wait_send()
 
 
@@ -559,19 +608,23 @@
             pltpu.VMEM(kind.shape, jnp.int32),
             pltpu.SemaphoreType.DMA((4,)),
             pltpu.VMEM((peers,) + moved.shape[1:], real),
-            pltpu.VMEM((peers,) + moved.shape[1:], real),
-            pltpu.VMEM((blocks,) + moved.shape[1:], real),
+            pltpu.VMEM((peers, 4, layers), real),
+            pltpu.VMEM((peers, 4, layers), real),
+            pltpu.VMEM((peers, 4, moved.shape[2] - 2 * layers), real),
+            pltpu.VMEM((blocks, 4, layers), real),
+            pltpu.VMEM((blocks, 4, layers), real),
+            pltpu.VMEM((blocks, 4, moved.shape[2] - 2 * layers), real),
             pltpu.VMEM((2, blocks, 4, layers), real),
             pltpu.VMEM((extent_x, 2) + tile, real),
             pltpu.VMEM((2, HALO) + tile, real),
             pltpu.VMEM((2, extent_x // HALO, 3) + tile, real),
             pltpu.VMEM((2, extent_x // HALO + 2, 3) + tile, real),
-            pltpu.VMEM((2, 5 * planes // 8) + tile, real),
-            pltpu.VMEM((2, 5 * planes // 8) + tile, real),
-            pltpu.SemaphoreType.DMA((peers,)),
-            pltpu.SemaphoreType.DMA((peers,)),
-            pltpu.SemaphoreType.DMA((18,)),
-            pltpu.SemaphoreType.DMA((18,)),
+            pltpu.VMEM((2, planes // 8, 5) + tile, real),
+            pltpu.VMEM((2, planes // 8, 5) + tile, real),
+            pltpu.SemaphoreType.DMA((3, peers)),
+            pltpu.SemaphoreType.DMA((3, peers)),
+            pltpu.SemaphoreType.DMA((24,)),
+            pltpu.SemaphoreType.DMA((24,)),
         ],
         compiler_params=pltpu.CompilerParams(
             collective_id=0, has_side_effects=True, vmem_limit_bytes=60 * 1024 * 1024

time: 36.5 us -> 50.9 us (1.39)
  Pallas kernels: 36.3 us -> 50.7 us
    pallas_call x1, Pallas kernels: 9.73 us -> 25 us  [lattice(): pl.pallas_call(lattice_kernel, out_shape=jax.ShapeDtypeStruct((19,) + tup...]
    pallas_call x1, Pallas kernels: 26.6 us -> 25.8 us  [gathered(): pl.pallas_call(gather_kernel, out_shape=jax.ShapeDtypeStruct((5, planes)...]
where the time goes in v4:
time: 50.9 us; the launch traced here: 50.7 us
  Pallas kernels  50.7 us (100%)
    pallas_call x1, Pallas kernels, gathered(): pl.pallas_call(gather_kernel, out_shape=jax.ShapeDtypeStruct((5, planes)...  25.8 us
    pallas_call x1, Pallas kernels, lattice(): pl.pallas_call(lattice_kernel, out_shape=jax.ShapeDtypeStruct((19,) + tup...  25 us

profile of v4, /device:TPU:1, one launch (start us, length us, event | category | flops | bytes accessed | tf_op | source)
XLA Modules:
  0.0 50.7 jit_solution(15983789122420799250)
XLA Ops:
  0.0 25.8 %gather.1.fields_in = f32[5,24,8,128]{3,2,1,0:T(8,128)} custom-call(f32[4,4,4096]{2,1,0:T(4,128)} %bitcast.3, s32[4]{0:T(128)} %bitcast.4, s32[2]{0:T(128)} %bitcast.5, s32[16,16,32]{2,1,0:T(8,128)} %kind_in.1), custom_call_target="tpu_custom_call" | custom-call | tf_op jit(solution)/shard_map/gather/pallas_call | solution.py:599
  25.8 25.0 %lattice.1 = f32[19,16,16,32]{3,2,1,0:T(8,128)} custom-call(f32[5,24,8,128]{3,2,1,0:T(8,128)} %gather.1.fields_in), custom_call_target="tpu_custom_call" | custom-call | tf_op jit(solution)/shard_map/lattice/pallas_call | solution.py:199

commit v5 on v4

--- a/solution.py
+++ b/solution.py
@@ -54,14 +54,18 @@
     return plane
 
 
-def unrolled(count, group, body):
+def unrolled(count, group, body, before=None, after=None):
     def several(sites):
         stores = [entry for site in sites for entry in body(site)]
         for ref, index, value in stores:
             ref[index] = value
 
     def step(first, carry):
+        if before is not None:
+            before(first)
         several([first * group + k for k in range(group)])
+        if after is not None:
+            after(first)
         return carry
 
     whole = count // group
@@ -129,27 +133,25 @@
 def lattice_kernel(fields_in, out, fields_ref, result, first, second, in_sem, out_sem):
     planes = fields_ref.shape[1]
     extent_x, extent_y, extent_z = out.shape[1:]
-    count = in_sem.shape[0]
-    cuts = [pl.ds(i * (planes // count), planes // count) for i in range(count)]
-    loads = [
-        pltpu.make_async_copy(fields_in.at[:, cut], fields_ref.at[:, cut], in_sem.at[i])
-        for i, cut in enumerate(cuts)
-    ]
-    for load in loads:
-        load.start()
+
+    def load(i):
+        cut = pl.ds(2 * i, 2)
+        return pltpu.make_async_copy(fields_in.at[:, cut], fields_ref.at[:, cut], in_sem.at[i])
+
+    def save(i):
+        cut = pl.ds(2 * i, 2)
+        return pltpu.make_async_copy(result.at[:, cut], out.at[:, cut], out_sem.at[i])
+
+    for i in range(planes // 2):
+        load(i).start()
     stride = extent_z + 2 * HALO
     rows = row_ids()
 
-    def begin(x, offset):
-        x = x + offset
+    def begin(x):
         fields = [fields_ref[i, x] for i in range(5)]
         return [(first, (i, x), m) for i, m in enumerate(start_plane(fields, fields[4]))]
 
-    for i, load in enumerate(loads):
-        load.wait()
-        unrolled(
-            planes // count, 3, functools.partial(begin, offset=i * (planes // count))
-        )
+    unrolled(planes, 2, begin, before=lambda i: load(i).wait())
     source, target = first, second
     for step in range(1, STEPS):
 
@@ -162,11 +164,10 @@
             updated = collide_plane(pulled, fields_ref[4, x])
             return [(target, (i, x), member) for i, member in enumerate(updated)]
 
-        unrolled(planes - 2 * step, 4, advance)
+        unrolled(planes - 2 * step, 2, advance)
         source, target = target, source
 
-    def finish(x, offset):
-        x = x + offset
+    def finish(x):
         stores = []
         for i, v in enumerate(VELOCITIES):
             plane = source[i, x + HALO - v[0]]
@@ -180,18 +181,9 @@
                 stores.append((result, cut, part[:, :extent_z]))
         return stores
 
-    count = out_sem.shape[0]
-    saves = []
-    for i in range(count):
-        length = extent_x // count
-        unrolled(length, 4, functools.partial(finish, offset=i * length))
-        cut = pl.ds(i * length, length)
-        saves.append(
-            pltpu.make_async_copy(result.at[:, cut], out.at[:, cut], out_sem.at[i])
-        )
-        saves[-1].start()
-    for save in saves:
-        save.wait()
+    unrolled(extent_x, 2, finish, after=lambda i: save(i).start())
+    for i in range(extent_x // 2):
+        save(i).wait()
 
 
 def lattice(fields, extents):
@@ -206,8 +198,8 @@
             pltpu.VMEM((19,) + tuple(extents), jnp.float32),
             pltpu.VMEM((19, planes, SUBLANES, LANES), jnp.float32),
             pltpu.VMEM((19, planes, SUBLANES, LANES), jnp.float32),
-            pltpu.SemaphoreType.DMA((4,)),
-            pltpu.SemaphoreType.DMA((4,)),
+            pltpu.SemaphoreType.DMA((planes // 2,)),
+            pltpu.SemaphoreType.DMA((extents[0] // 2,)),
         ],
         compiler_params=pltpu.CompilerParams(vmem_limit_bytes=60 * 1024 * 1024),
         name="lattice",

time: 50.9 us -> 35.6 us (0.70)
  Pallas kernels: 50.7 us -> 35.4 us
    pallas_call x1, Pallas kernels: 25 us -> 9.63 us  [lattice(): pl.pallas_call(lattice_kernel, out_shape=jax.ShapeDtypeStruct((19,) + tup...]
where the time goes in v5:
time: 35.6 us; the launch traced here: 35.4 us
  Pallas kernels  35.4 us (99%)
    pallas_call x1, Pallas kernels, gathered(): pl.pallas_call(gather_kernel, out_shape=jax.ShapeDtypeStruct((5, planes)...  25.8 us
    pallas_call x1, Pallas kernels, lattice(): pl.pallas_call(lattice_kernel, out_shape=jax.ShapeDtypeStruct((19,) + tup...  9.63 us

profile of v5, /device:TPU:1, one launch (start us, length us, event | category | flops | bytes accessed | tf_op | source)
XLA Modules:
  0.0 35.4 jit_solution(15612417254348900950)
XLA Ops:
  0.0 25.8 %gather.1.fields_in = f32[5,24,8,128]{3,2,1,0:T(8,128)} custom-call(f32[4,4,4096]{2,1,0:T(4,128)} %bitcast.3, s32[4]{0:T(128)} %bitcast.4, s32[2]{0:T(128)} %bitcast.5, s32[16,16,32]{2,1,0:T(8,128)} %kind_in.1), custom_call_target="tpu_custom_call" | custom-call | tf_op jit(solution)/shard_map/gather/pallas_call | solution.py:591
  25.8 9.6 %lattice.1 = f32[19,16,16,32]{3,2,1,0:T(8,128)} custom-call(f32[5,24,8,128]{3,2,1,0:T(8,128)} %gather.1.fields_in), custom_call_target="tpu_custom_call" | custom-call | tf_op jit(solution)/shard_map/lattice/pallas_call | solution.py:191

commit v6 on v5

--- a/solution.py
+++ b/solution.py
@@ -485,7 +485,7 @@
         def lay(x):
             return lay_fields(lambda block, cut: source[block, :, cut], x, first_x + x)
 
-        unrolled(count, 4, lay)
+        unrolled(count, 2, lay)
 
     choose(0, chosen_low)
     choose(1, chosen_high)
@@ -509,7 +509,7 @@
             )
             return stores + [(out_ref, (4, first_x + x), kind_x[side, x])]
 
-        unrolled(HALO, 4, lay_side)
+        unrolled(HALO, 2, lay_side)
 
     choose(2, chosen_mid)
     lay_own(chosen_mid, extent_x - 2 * HALO, 2 * HALO)

time: 35.6 us -> 36.8 us (1.034)
  Pallas kernels: 35.4 us -> 36.6 us
    pallas_call x1, Pallas kernels: 25.8 us -> 27 us  [gathered(): pl.pallas_call(gather_kernel, out_shape=jax.ShapeDtypeStruct((5, planes)...]
where the time goes in v6:
time: 36.8 us; the launch traced here: 36.6 us
  Pallas kernels  36.6 us (99%)
    pallas_call x1, Pallas kernels, gathered(): pl.pallas_call(gather_kernel, out_shape=jax.ShapeDtypeStruct((5, planes)...  27 us
    pallas_call x1, Pallas kernels, lattice(): pl.pallas_call(lattice_kernel, out_shape=jax.ShapeDtypeStruct((19,) + tup...  9.63 us

profile of v6, /device:TPU:1, one launch (start us, length us, event | category | flops | bytes accessed | tf_op | source)
XLA Modules:
  0.0 36.6 jit_solution(4756987184893804352)
XLA Ops:
  0.0 27.0 %gather.1.fields_in = f32[5,24,8,128]{3,2,1,0:T(8,128)} custom-call(f32[4,4,4096]{2,1,0:T(4,128)} %bitcast.3, s32[4]{0:T(128)} %bitcast.4, s32[2]{0:T(128)} %bitcast.5, s32[16,16,32]{2,1,0:T(8,128)} %kind_in.1), custom_call_target="tpu_custom_call" | custom-call | tf_op jit(solution)/shard_map/gather/pallas_call | solution.py:591
  27.0 9.6 %lattice.1 = f32[19,16,16,32]{3,2,1,0:T(8,128)} custom-call(f32[5,24,8,128]{3,2,1,0:T(8,128)} %gather.1.fields_in), custom_call_target="tpu_custom_call" | custom-call | tf_op jit(solution)/shard_map/lattice/pallas_call | solution.py:191

commit v7 on v5

--- a/solution.py
+++ b/solution.py
@@ -432,7 +432,7 @@
         plane = grouped(parts[0], parts[1], rows, lanes, stride)
         return [(out_ref, (4, x + HALO), plane)]
 
-    unrolled(extent_x, 4, lay_kind)
+    unrolled(extent_x, 8, lay_kind)
     kind_copies = halo(
         "gx",
         0,
@@ -485,7 +485,7 @@
         def lay(x):
             return lay_fields(lambda block, cut: source[block, :, cut], x, first_x + x)
 
-        unrolled(count, 4, lay)
+        unrolled(count, 8, lay)
 
     choose(0, chosen_low)
     choose(1, chosen_high)

time: 35.6 us -> 35.7 us (level)
  no operation moved by 1% of the time
where the time goes in v7:
time: 35.7 us; the launch traced here: 35.5 us
  Pallas kernels  35.4 us (99%)
    pallas_call x1, Pallas kernels, gathered(): pl.pallas_call(gather_kernel, out_shape=jax.ShapeDtypeStruct((5, planes)...  25.8 us
    pallas_call x1, Pallas kernels, lattice(): pl.pallas_call(lattice_kernel, out_shape=jax.ShapeDtypeStruct((19,) + tup...  9.63 us

profile of v7, /device:TPU:1, one launch (start us, length us, event | category | flops | bytes accessed | tf_op | source)
XLA Modules:
  0.0 35.5 jit_solution(16613800210091506719)
XLA Ops:
  0.0 25.8 %gather.1.fields_in = f32[5,24,8,128]{3,2,1,0:T(8,128)} custom-call(f32[4,4,4096]{2,1,0:T(4,128)} %bitcast.3, s32[4]{0:T(128)} %bitcast.4, s32[2]{0:T(128)} %bitcast.5, s32[16,16,32]{2,1,0:T(8,128)} %kind_in.1), custom_call_target="tpu_custom_call" | custom-call | tf_op jit(solution)/shard_map/gather/pallas_call | solution.py:591
  25.8 9.6 %lattice.1 = f32[19,16,16,32]{3,2,1,0:T(8,128)} custom-call(f32[5,24,8,128]{3,2,1,0:T(8,128)} %gather.1.fields_in), custom_call_target="tpu_custom_call" | custom-call | tf_op jit(solution)/shard_map/lattice/pallas_call | solution.py:191
